TPU v7x, 32 devices: a whole 2x2x4 slice. The times are simulated.
32 devices in a mesh: shard: 2 (over x), ctx: 4 (over y, core), tp: 4 (over z).
Axes of the slice: x: 2, y: 2, z: 4, core: 2. Of those that a mesh axis runs over, the one named last changes fastest.
Arguments:
- hidden_in: bfloat16 [2, 768, 1024], P('shard', 'ctx'), may hold values from -6 to 6
- seg_ids: int32 [2, 768], P('shard'), may hold values from 0 to 3, as said below
- attn_in: bfloat16 [2, 3, 1024, 1024], P(None, None, ('shard', 'ctx'), 'tp'), may hold values from -0.1875 to 0.1875
- attn_bias: bfloat16 [2, 2, 4, 256], P(None, None, 'tp', ('shard', 'ctx')), may hold values from -3 to 3
- attn_out: bfloat16 [2, 1024, 1024], P(None, 'tp', ('shard', 'ctx')), may hold values from -0.75 to 0.75
- ff_in: bfloat16 [2, 1024, 4096], P(None, ('shard', 'ctx'), 'tp'), may hold values from -0.1875 to 0.1875
- ff_bias: bfloat16 [2, 4, 1024], P(None, 'tp', ('shard', 'ctx')), may hold values from -3 to 3
- ff_out: bfloat16 [2, 4096, 1024], P(None, 'tp', ('shard', 'ctx')), may hold values from -0.09375 to 0.09375
- gains: bfloat16 [2, 2, 1024], P(None, None, ('shard', 'ctx')), may hold values from 0.5 to 1.5
- shifts: bfloat16 [2, 4, 1024], P(None, None, ('shard', 'ctx')), may hold values from -3 to 3
- cotangent: bfloat16 [2, 768, 1024], P('shard', 'ctx'), may hold values from -6 to 6
Outputs:
- hidden_out: bfloat16 [2, 768, 1024], P('shard', 'ctx')
- grad_in: float32 [2, 768, 1024], P('shard', 'ctx')
- grad_attn_in: float32 [2, 3, 1024, 1024], P(None, None, ('shard', 'ctx'), 'tp')
- grad_attn_bias: float32 [2, 2, 4, 256], P(None, None, 'tp', ('shard', 'ctx'))
- grad_attn_out: float32 [2, 1024, 1024], P(None, 'tp', ('shard', 'ctx'))
- grad_ff_in: float32 [2, 1024, 4096], P(None, ('shard', 'ctx'), 'tp')
- grad_ff_bias: float32 [2, 4, 1024], P(None, 'tp', ('shard', 'ctx'))
- grad_ff_out: float32 [2, 4096, 1024], P(None, 'tp', ('shard', 'ctx'))
- grad_gains: float32 [2, 2, 1024], P(None, None, ('shard', 'ctx'))
- grad_shifts: float32 [2, 4, 1024], P(None, None, ('shard', 'ctx'))
Inputs may be any that keep to these rules, and one draw needn't show every extreme that they name: `seg_ids`: each row holds four sequences numbered 0 to 3 in order, each at least one position long; sequence 1 holds exactly 512 positions and reaches from the first 192 positions of its row into the last 192.
All inputs are finite; a program needn't handle non-finite values.
Results may differ from a plain program's by a relative error of at most 0.02.
Values may be sent and summed in bfloat16 or wider, within the bound.
No kernel may reach another device: no remote copies, remote signals or barrier semaphores. Data moves between devices by JAX's collectives and lax.ppermute only.
A program may use at most 128 MiB of HBM per device.

v0:
```python
import jax
import jax.numpy as jnp
from jax import lax
from jax.sharding import PartitionSpec as P

HD = 64


SCORE_FLOOR = -1e30


def gelu_exact(values):
    return jax.nn.gelu(values, approximate=False)


def normalize(values, gain, shift):
    centre = values - jnp.mean(values, axis=-1, keepdims=True)
    scale_inv = lax.rsqrt(jnp.mean(centre * centre, axis=-1, keepdims=True) + 1e-12)
    normed = centre * scale_inv
    return (normed * gain + shift, normed, scale_inv)


def norm_back(grad_out, normed, scale_inv, gain):
    scaled = grad_out * gain
    grad_rows = scale_inv * (
        scaled
        - jnp.mean(scaled, axis=-1, keepdims=True)
        - normed * jnp.mean(scaled * normed, axis=-1, keepdims=True)
    )
    return (grad_rows, jnp.sum(grad_out * normed, axis=0), jnp.sum(grad_out, axis=0))


def tensor_sum(term):
    return lax.psum(term, "tp")


def tensor_back_sum(term):
    return lax.psum(term, "tp")


def fetch_forward(attn_in, attn_bias, attn_out, ff_in, ff_bias, ff_out, gains, shifts, layer_index):
    return (
        lax.all_gather(attn_in[layer_index], ("shard", "ctx"), axis=1, tiled=True),
        lax.all_gather(attn_bias[layer_index], ("shard", "ctx"), axis=2, tiled=True),
        lax.all_gather(attn_out[layer_index], ("shard", "ctx"), axis=1, tiled=True),
        lax.all_gather(ff_in[layer_index], ("shard", "ctx"), axis=0, tiled=True),
        lax.all_gather(ff_bias[layer_index], ("shard", "ctx"), axis=1, tiled=True),
        lax.all_gather(ff_out[layer_index], ("shard", "ctx"), axis=1, tiled=True),
        lax.all_gather(gains[layer_index], ("shard", "ctx"), axis=1, tiled=True),
        lax.all_gather(shifts[layer_index], ("shard", "ctx"), axis=1, tiled=True),
    )


def fetch_backward(
    attn_in, attn_bias, attn_out, ff_in, ff_bias, ff_out, gains, shifts, layer_index
):
    return (
        lax.all_gather(attn_in[layer_index], ("shard", "ctx"), axis=1, tiled=True),
        lax.all_gather(attn_bias[layer_index], ("shard", "ctx"), axis=2, tiled=True),
        lax.all_gather(attn_out[layer_index], ("shard", "ctx"), axis=1, tiled=True),
        lax.all_gather(ff_in[layer_index], ("shard", "ctx"), axis=0, tiled=True),
        lax.all_gather(ff_bias[layer_index], ("shard", "ctx"), axis=1, tiled=True),
        lax.all_gather(ff_out[layer_index], ("shard", "ctx"), axis=1, tiled=True),
        lax.all_gather(gains[layer_index], ("shard", "ctx"), axis=1, tiled=True),
        lax.all_gather(shifts[layer_index], ("shard", "ctx"), axis=1, tiled=True),
    )


def score_block(queries, keys_all, same_seq, pack_count, tok_dev, heads_here):
    query_heads = queries.reshape(pack_count, tok_dev, heads_here, HD)
    key_heads = keys_all.reshape(pack_count, -1, heads_here, HD)
    scores = jnp.einsum(
        "pqhd,pkhd->phqk", query_heads, key_heads, preferred_element_type=jnp.float32
    ) * HD ** (-0.5)
    return jnp.where(same_seq[:, None], scores, SCORE_FLOOR)


def forward_layer(inputs, pieces, same_seq, pack_count, tok_dev):
    w_qkv, bias_qv, w_out, w_up, bias_up, w_down, gain_pair, shift_four = pieces
    local_width = w_qkv.shape[2]
    heads_here = local_width // HD
    row_count = inputs.shape[0]
    gain_f = gain_pair.astype(jnp.float32)
    shift_f = shift_four.astype(jnp.float32)
    inputs_low = inputs.astype(jnp.bfloat16)
    projected = jnp.einsum("rd,cde->cre", inputs_low, w_qkv, preferred_element_type=jnp.float32)
    bias_flat = bias_qv.reshape(2, local_width).astype(jnp.float32)
    queries = (projected[0] + bias_flat[0]).astype(jnp.bfloat16)
    keys_own = projected[1].astype(jnp.bfloat16)
    values_own = (projected[2] + bias_flat[1]).astype(jnp.bfloat16)
    keys_all, values_all = (
        lax.all_gather(
            keys_own.reshape(pack_count, tok_dev, local_width), "ctx", axis=1, tiled=True
        ),
        lax.all_gather(
            values_own.reshape(pack_count, tok_dev, local_width), "ctx", axis=1, tiled=True
        ),
    )
    scores = score_block(queries, keys_all, same_seq, pack_count, tok_dev, heads_here)
    top_score = jnp.max(scores, axis=-1, keepdims=True)
    exponent = jnp.exp(scores - top_score)
    totals = jnp.sum(exponent, axis=-1, keepdims=True)
    prob_low = (exponent / totals).astype(jnp.bfloat16)
    log_total = top_score + jnp.log(totals)
    value_heads = values_all.reshape(pack_count, -1, heads_here, HD)
    context = jnp.einsum(
        "phqk,pkhd->pqhd", prob_low, value_heads, preferred_element_type=jnp.float32
    )
    context = context.reshape(row_count, local_width).astype(jnp.bfloat16)
    attn_output = (
        tensor_sum(jnp.dot(context, w_out, preferred_element_type=jnp.float32)) + shift_f[0]
    )
    hidden, normed_one, inv_one = normalize(inputs + attn_output, gain_f[0], shift_f[1])
    hidden_low = hidden.astype(jnp.bfloat16)
    up_proj = jnp.dot(hidden_low, w_up, preferred_element_type=jnp.float32) + bias_up.reshape(
        -1
    ).astype(jnp.float32)
    active = gelu_exact(up_proj).astype(jnp.bfloat16)
    ff_output = tensor_sum(jnp.dot(active, w_down, preferred_element_type=jnp.float32)) + shift_f[2]
    output, normed_two, inv_two = normalize(hidden + ff_output, gain_f[1], shift_f[3])
    kept_state = (
        inputs_low,
        queries,
        keys_all,
        values_all,
        log_total,
        context,
        normed_one,
        inv_one,
        hidden_low,
        up_proj,
        active,
        normed_two,
        inv_two,
    )
    return (output, kept_state)


def backward_layer(grad_out, kept_state, pieces, same_seq, pack_count, tok_dev):
    (
        inputs_low,
        queries,
        keys_all,
        values_all,
        log_total,
        context,
        normed_one,
        inv_one,
        hidden_low,
        up_proj,
        active,
        normed_two,
        inv_two,
    ) = kept_state
    w_qkv, bias_qv, w_out, w_up, bias_up, w_down, gain_pair, shift_four = pieces
    local_width = w_qkv.shape[2]
    heads_here = local_width // HD
    row_count = grad_out.shape[0]
    gain_f = gain_pair.astype(jnp.float32)
    grad_two, grad_gain_two, grad_shift_three = norm_back(grad_out, normed_two, inv_two, gain_f[1])
    grad_shift_two = jnp.sum(grad_two, axis=0)
    grad_ff_low = grad_two.astype(jnp.bfloat16)
    grad_down = jnp.einsum("rf,rd->fd", active, grad_ff_low, preferred_element_type=jnp.float32)
    grad_active = jnp.einsum("rd,fd->rf", grad_ff_low, w_down, preferred_element_type=jnp.float32)
    grad_up_proj = jax.vjp(gelu_exact, up_proj)[1](grad_active)[0].astype(jnp.bfloat16)
    grad_bias_up = jnp.sum(grad_up_proj.astype(jnp.float32), axis=0)
    grad_w_up = jnp.einsum(
        "rd,rf->df", hidden_low, grad_up_proj, preferred_element_type=jnp.float32
    )
    grad_hidden = grad_two + tensor_back_sum(
        jnp.einsum("rf,df->rd", grad_up_proj, w_up, preferred_element_type=jnp.float32)
    )
    grad_one, grad_gain_one, grad_shift_one = norm_back(grad_hidden, normed_one, inv_one, gain_f[0])
    grad_shift_zero = jnp.sum(grad_one, axis=0)
    grad_attn_low = grad_one.astype(jnp.bfloat16)
    grad_w_out = jnp.einsum("re,rd->ed", context, grad_attn_low, preferred_element_type=jnp.float32)
    grad_context = jnp.einsum(
        "rd,ed->re", grad_attn_low, w_out, preferred_element_type=jnp.float32
    ).astype(jnp.bfloat16)
    scores = score_block(queries, keys_all, same_seq, pack_count, tok_dev, heads_here)
    prob_table = jnp.exp(scores - log_total)
    prob_low = prob_table.astype(jnp.bfloat16)
    query_heads = queries.reshape(pack_count, tok_dev, heads_here, HD)
    key_heads = keys_all.reshape(pack_count, -1, heads_here, HD)
    value_heads = values_all.reshape(pack_count, -1, heads_here, HD)
    grad_ctx_heads = grad_context.reshape(pack_count, tok_dev, heads_here, HD)
    grad_probs = jnp.einsum(
        "pqhd,pkhd->phqk", grad_ctx_heads, value_heads, preferred_element_type=jnp.float32
    )
    grad_values_all = jnp.einsum(
        "phqk,pqhd->pkhd", prob_low, grad_ctx_heads, preferred_element_type=jnp.float32
    )
    row_dot = jnp.sum(grad_probs * prob_table, axis=-1, keepdims=True)
    grad_scores = (prob_table * (grad_probs - row_dot)).astype(jnp.bfloat16)
    grad_queries = jnp.einsum(
        "phqk,pkhd->pqhd", grad_scores, key_heads, preferred_element_type=jnp.float32
    ) * HD ** (-0.5)
    grad_queries = grad_queries.reshape(row_count, local_width).astype(jnp.bfloat16)
    grad_keys_all = jnp.einsum(
        "phqk,pqhd->pkhd", grad_scores, query_heads, preferred_element_type=jnp.float32
    ) * HD ** (-0.5)
    grad_keys, grad_values = (
        lax.psum_scatter(
            grad_keys_all.reshape(pack_count, -1, local_width),
            "ctx",
            scatter_dimension=1,
            tiled=True,
        ),
        lax.psum_scatter(
            grad_values_all.reshape(pack_count, -1, local_width),
            "ctx",
            scatter_dimension=1,
            tiled=True,
        ),
    )
    grad_keys = grad_keys.reshape(row_count, local_width).astype(jnp.bfloat16)
    grad_values = grad_values.reshape(row_count, local_width).astype(jnp.bfloat16)
    grad_stack = jnp.stack([grad_queries, grad_keys, grad_values])
    grad_w_qkv = jnp.einsum(
        "rd,cre->cde", inputs_low, grad_stack, preferred_element_type=jnp.float32
    )
    grad_bias_qv = jnp.stack(
        [
            jnp.sum(grad_queries.astype(jnp.float32), axis=0),
            jnp.sum(grad_values.astype(jnp.float32), axis=0),
        ]
    ).reshape(bias_qv.shape)
    grad_inputs = grad_one + tensor_back_sum(
        jnp.einsum("cre,cde->rd", grad_stack, w_qkv, preferred_element_type=jnp.float32)
    )
    grad_terms = (
        grad_w_qkv,
        grad_bias_qv,
        grad_w_out,
        grad_w_up,
        grad_bias_up.reshape(bias_up.shape),
        grad_down,
        jnp.stack([grad_gain_one, grad_gain_two]),
        jnp.stack([grad_shift_zero, grad_shift_one, grad_shift_two, grad_shift_three]),
    )
    return (grad_inputs, grad_terms)


def stack_member(layer_grads, member):
    return jnp.stack([entry[member] for entry in layer_grads])


def shards(
    hidden_in,
    seg_ids,
    attn_in,
    attn_bias,
    attn_out,
    ff_in,
    ff_bias,
    ff_out,
    gains,
    shifts,
    cotangent,
):
    pack_count, tok_dev, model_width = hidden_in.shape
    layer_count = attn_in.shape[0]
    ctx_index = lax.axis_index("ctx")
    query_segs = lax.dynamic_slice_in_dim(seg_ids, ctx_index * tok_dev, tok_dev, 1)
    same_seq = query_segs[:, :, None] == seg_ids[:, None, :]
    current = hidden_in.reshape(-1, model_width).astype(jnp.float32)
    stored = []
    for layer_index in range(layer_count):
        pieces = fetch_forward(
            attn_in, attn_bias, attn_out, ff_in, ff_bias, ff_out, gains, shifts, layer_index
        )
        current, kept_state = forward_layer(current, pieces, same_seq, pack_count, tok_dev)
        stored.append(kept_state)
    hidden_out = current.astype(jnp.bfloat16).reshape(pack_count, tok_dev, model_width)
    grad_current = cotangent.reshape(-1, model_width).astype(jnp.float32)
    layer_grads = [None] * layer_count
    for layer_index in reversed(range(layer_count)):
        pieces = fetch_backward(
            attn_in, attn_bias, attn_out, ff_in, ff_bias, ff_out, gains, shifts, layer_index
        )
        grad_current, grad_terms = backward_layer(
            grad_current, stored[layer_index], pieces, same_seq, pack_count, tok_dev
        )
        layer_grads[layer_index] = (
            lax.psum_scatter(
                grad_terms[0].astype(jnp.bfloat16),
                ("shard", "ctx"),
                scatter_dimension=1,
                tiled=True,
            ).astype(jnp.float32),
            lax.psum_scatter(
                grad_terms[1].astype(jnp.bfloat16),
                ("shard", "ctx"),
                scatter_dimension=2,
                tiled=True,
            ).astype(jnp.float32),
            lax.psum_scatter(
                grad_terms[2].astype(jnp.bfloat16),
                ("shard", "ctx"),
                scatter_dimension=1,
                tiled=True,
            ).astype(jnp.float32),
            lax.psum_scatter(
                grad_terms[3].astype(jnp.bfloat16),
                ("shard", "ctx"),
                scatter_dimension=0,
                tiled=True,
            ).astype(jnp.float32),
            lax.psum_scatter(
                grad_terms[4].astype(jnp.bfloat16),
                ("shard", "ctx"),
                scatter_dimension=1,
                tiled=True,
            ).astype(jnp.float32),
            lax.psum_scatter(
                grad_terms[5].astype(jnp.bfloat16),
                ("shard", "ctx"),
                scatter_dimension=1,
                tiled=True,
            ).astype(jnp.float32),
            lax.psum_scatter(
                grad_terms[6].astype(jnp.bfloat16),
                ("shard", "ctx"),
                scatter_dimension=1,
                tiled=True,
            ).astype(jnp.float32),
            lax.psum_scatter(
                grad_terms[7].astype(jnp.bfloat16),
                ("shard", "ctx"),
                scatter_dimension=1,
                tiled=True,
            ).astype(jnp.float32),
        )
    results = tuple((stack_member(layer_grads, member) for member in range(8)))
    grad_in = grad_current.reshape(pack_count, tok_dev, model_width)
    return (
        hidden_out,
        grad_in,
        results[0],
        results[1],
        results[2],
        results[3],
        results[4],
        results[5],
        results[6],
        results[7],
    )


def solution(mesh):
    in_specs = (
        P("shard", "ctx", None),
        P("shard", None),
        P(None, None, ("shard", "ctx"), "tp"),
        P(None, None, "tp", ("shard", "ctx")),
        P(None, "tp", ("shard", "ctx")),
        P(None, ("shard", "ctx"), "tp"),
        P(None, "tp", ("shard", "ctx")),
        P(None, "tp", ("shard", "ctx")),
        P(None, None, ("shard", "ctx")),
        P(None, None, ("shard", "ctx")),
        P("shard", "ctx", None),
    )
    out_specs = (
        P("shard", "ctx", None),
        P("shard", "ctx", None),
        P(None, None, ("shard", "ctx"), "tp"),
        P(None, None, "tp", ("shard", "ctx")),
        P(None, "tp", ("shard", "ctx")),
        P(None, ("shard", "ctx"), "tp"),
        P(None, "tp", ("shard", "ctx")),
        P(None, "tp", ("shard", "ctx")),
        P(None, None, ("shard", "ctx")),
        P(None, None, ("shard", "ctx")),
    )
    return jax.shard_map(shards, mesh=mesh, in_specs=in_specs, out_specs=out_specs, check_vma=False)
```

profile of v0, /device:TPU:0, one launch (start us, length us, event | category | flops | bytes accessed | tf_op | source)
XLA Modules:
  0.0 1385.6 jit_solution(7861883346208705388)
XLA Ops:
  107.3 27.6 %all-gather.25.cloned.1.call-done = bf16[1,1024,1024]{2,1,0:T(8,128)(2,1)} async-done(((bf16[1,128,1024]{2,1,0:T(8,128)(2,1)}), bf16[1,1024,1024]{2,1,0:T(8,128)(2,1)}) %all-gather.25.cloned.1.call-update) | async-done | bytes 2097168 | tf_op jit(solution)/shard_map/all_gather | solution.py:46
  139.5 25.9 %all-gather.27.cloned.1.call-done = bf16[1,1024,1024]{2,1,0:T(8,128)(2,1)} async-done(((bf16[1,1024,128]{2,1,0:T(8,128)(2,1)}), bf16[1,1024,1024]{2,1,0:T(8,128)(2,1)}) %all-gather.27.cloned.1.call-update) | async-done | bytes 2097168 | tf_op jit(solution)/shard_map/all_gather | solution.py:48
  314.5 26.3 %all-gather.31.cloned.1.call-done = bf16[1,1024,1024]{2,1,0:T(8,128)(2,1)} async-done(((bf16[1,128,1024]{2,1,0:T(8,128)(2,1)}), bf16[1,1024,1024]{2,1,0:T(8,128)(2,1)}) %all-gather.31.cloned.1.call-update) | async-done | bytes 2097168 | tf_op jit(solution)/shard_map/all_gather | solution.py:46
  374.2 43.6 %all-reduce.15.cloned.1.call-done = f32[192,1024]{1,0:T(8,128)} async-done(((f32[192,1024]{1,0:T(8,128)}), f32[192,1024]{1,0:T(8,128)}) %all-reduce.15.cloned.1.call-update) | async-done | bytes 786448 | tf_op jit(solution)/shard_map/psum | solution.py:34
  428.9 42.4 %all-reduce.17.cloned.1.call-done = f32[192,1024]{1,0:T(8,128)} async-done(((f32[192,1024]{1,0:T(8,128)}), f32[192,1024]{1,0:T(8,128)}) %all-reduce.17.cloned.1.call-update) | async-done | bytes 786448 | tf_op jit(solution)/shard_map/psum | solution.py:38
  540.8 43.5 %all-reduce.19.cloned.1.call-done = f32[192,1024]{1,0:T(8,128)} async-done(((f32[192,1024]{1,0:T(8,128)}), f32[192,1024]{1,0:T(8,128)}) %all-reduce.19.cloned.1.call-update) | async-done | bytes 786448 | tf_op jit(solution)/shard_map/psum | solution.py:38
  595.0 42.4 %all-reduce.21.cloned.1.call-done = f32[192,1024]{1,0:T(8,128)} async-done(((f32[192,1024]{1,0:T(8,128)}), f32[192,1024]{1,0:T(8,128)}) %all-reduce.21.cloned.1.call-update) | async-done | bytes 786448 | tf_op jit(solution)/shard_map/psum | solution.py:38
  706.8 28.2 %reduce-scatter.75.cloned.1.call-done = bf16[128,1]{1,0:T(8,128)(2,1)} async-done(((bf16[1024,1]{1,0:T(8,128)(2,1)}), bf16[128,1]{1,0:T(8,128)(2,1)}) %reduce-scatter.75.cloned.1.call-update) | async-done | bytes 272
  735.8 36.1 %reduce-scatter.83.cloned.1.call-done = bf16[128,2]{1,0:T(8,128)(2,1)} async-done(((bf16[1024,2]{1,0:T(8,128)(2,1)}), bf16[128,2]{1,0:T(8,128)(2,1)}) %reduce-scatter.83.cloned.1.call-update) | async-done | bytes 528
  772.7 35.7 %reduce-scatter.87.cloned.1.call-done = bf16[128,4]{1,0:T(8,128)(2,1)} async-done(((bf16[1024,4]{1,0:T(8,128)(2,1)}), bf16[128,4]{1,0:T(8,128)(2,1)}) %reduce-scatter.87.cloned.1.call-update) | async-done | bytes 1040
  809.3 37.3 %reduce-scatter.71.cloned.1.call-done = bf16[128,256]{1,0:T(8,128)(2,1)} async-done(((bf16[1024,256]{1,0:T(8,128)(2,1)}), bf16[128,256]{1,0:T(8,128)(2,1)}) %reduce-scatter.71.cloned.1.call-update) | async-done | bytes 65552
  847.5 35.3 %reduce-scatter.67.cloned.1.call-done = bf16[32,2]{1,0:T(8,128)(2,1)} async-done(((bf16[256,2]{1,0:T(8,128)(2,1)}), bf16[32,2]{1,0:T(8,128)(2,1)}) %reduce-scatter.67.cloned.1.call-update) | async-done | bytes 144
  883.6 44.1 %reduce-scatter.79.cloned.1.call-done = bf16[128,1024]{1,0:T(8,128)(2,1)} async-done(((bf16[1024,1024]{1,0:T(8,128)(2,1)}), bf16[128,1024]{1,0:T(8,128)(2,1)}) %reduce-scatter.79.cloned.1.call-update) | async-done | bytes 262160
  928.8 35.4 %reduce-scatter.73.cloned.1.call-done = bf16[128,1]{1,0:T(8,128)(2,1)} async-done(((bf16[1024,1]{1,0:T(8,128)(2,1)}), bf16[128,1]{1,0:T(8,128)(2,1)}) %reduce-scatter.73.cloned.1.call-update) | async-done | bytes 272
  965.6 35.6 %reduce-scatter.81.cloned.1.call-done = bf16[128,2]{1,0:T(8,128)(2,1)} async-done(((bf16[1024,2]{1,0:T(8,128)(2,1)}), bf16[128,2]{1,0:T(8,128)(2,1)}) %reduce-scatter.81.cloned.1.call-update) | async-done | bytes 528
  1002.6 35.1 %reduce-scatter.85.cloned.1.call-done = bf16[128,4]{1,0:T(8,128)(2,1)} async-done(((bf16[1024,4]{1,0:T(8,128)(2,1)}), bf16[128,4]{1,0:T(8,128)(2,1)}) %reduce-scatter.85.cloned.1.call-update) | async-done | bytes 1040
  1039.1 40.5 %reduce-scatter.63.cloned.1.call-done = bf16[128,768]{1,0:T(8,128)(2,1)} async-done(((bf16[1024,768]{1,0:T(8,128)(2,1)}), bf16[128,768]{1,0:T(8,128)(2,1)}) %reduce-scatter.63.cloned.1.call-update) | async-done | bytes 196624
  1080.9 36.9 %reduce-scatter.69.cloned.1.call-done = bf16[128,256]{1,0:T(8,128)(2,1)} async-done(((bf16[1024,256]{1,0:T(8,128)(2,1)}), bf16[128,256]{1,0:T(8,128)(2,1)}) %reduce-scatter.69.cloned.1.call-update) | async-done | bytes 65552
  1119.4 34.6 %reduce-scatter.65.cloned.1.call-done = bf16[32,2]{1,0:T(8,128)(2,1)} async-done(((bf16[256,2]{1,0:T(8,128)(2,1)}), bf16[32,2]{1,0:T(8,128)(2,1)}) %reduce-scatter.65.cloned.1.call-update) | async-done | bytes 144
  1155.4 43.4 %reduce-scatter.77.cloned.1.call-done = bf16[128,1024]{1,0:T(8,128)(2,1)} async-done(((bf16[1024,1024]{1,0:T(8,128)(2,1)}), bf16[128,1024]{1,0:T(8,128)(2,1)}) %reduce-scatter.77.cloned.1.call-update) | async-done | bytes 262160
  1200.9 42.4 %reduce-scatter.59.cloned.1.call-done = bf16[128,1024]{1,0:T(8,128)(2,1)} async-done(((bf16[1024,1024]{1,0:T(8,128)(2,1)}), bf16[128,1024]{1,0:T(8,128)(2,1)}) %reduce-scatter.59.cloned.1.call-update) | async-done | bytes 262160 | tf_op jit(solution)/shard_map/reduce_scatter | solution.py:303
  1243.3 44.9 %reduce-scatter.57.cloned.1.call-done = bf16[128,1024]{1,0:T(8,128)(2,1)} async-done(((bf16[1024,1024]{1,0:T(8,128)(2,1)}), bf16[128,1024]{1,0:T(8,128)(2,1)}) %reduce-scatter.57.cloned.1.call-update) | async-done | bytes 262160 | tf_op jit(solution)/shard_map/reduce_scatter | solution.py:303
  1290.3 44.4 %all-reduce.23.cloned.1.call-done = f32[192,1024]{1,0:T(8,128)} async-done(((f32[192,1024]{1,0:T(8,128)}), f32[192,1024]{1,0:T(8,128)}) %all-reduce.23.cloned.1.call-update) | async-done | bytes 786448 | tf_op jit(solution)/shard_map/psum | solution.py:38
  1336.8 39.0 %reduce-scatter.61.cloned.1.call-done = bf16[128,768]{1,0:T(8,128)(2,1)} async-done(((bf16[1024,768]{1,0:T(8,128)(2,1)}), bf16[128,768]{1,0:T(8,128)(2,1)}) %reduce-scatter.61.cloned.1.call-update) | async-done | bytes 196624
  (495 shorter events, 468.8 us)
Async XLA Ops:
  9.1 96.1 %all-reduce.9.cloned.1.call-start = ((), (), s32[]{:S(2)}) async-start(), calls=%async_computation.20 | async-start | bytes 1572864 | tf_op jit(solution)/shard_map/psum | solution.py:34
  63.2 102.2 %all-gather.27.cloned.1.call-start = ((), (), s32[]{:S(2)}) async-start(), calls=%async_computation.36 | async-start | bytes 2359296 | tf_op jit(solution)/shard_map/all_gather | solution.py:48
  65.2 147.1 %all-reduce.11.cloned.1.call-start = ((), (), s32[]{:S(2)}) async-start(), calls=%async_computation.21 | async-start | bytes 1572864 | tf_op jit(solution)/shard_map/psum | solution.py:34
  169.1 142.0 %all-reduce.13.cloned.1.call-start = ((), (), s32[]{:S(2)}) async-start(), calls=%async_computation.22 | async-start | bytes 1572864 | tf_op jit(solution)/shard_map/psum | solution.py:34
  267.9 103.0 %all-gather.33.cloned.1.call-start = ((), (), s32[]{:S(2)}) async-start(), calls=%async_computation.39 | async-start | bytes 2359296 | tf_op jit(solution)/shard_map/all_gather | solution.py:48
  268.7 149.2 %all-reduce.15.cloned.1.call-start = ((), (), s32[]{:S(2)}) async-start(), calls=%async_computation.23 | async-start | bytes 1572864 | tf_op jit(solution)/shard_map/psum | solution.py:34
  374.0 97.3 %all-reduce.17.cloned.1.call-start = ((), (), s32[]{:S(2)}) async-start(), calls=%async_computation.24 | async-start | bytes 1572864 | tf_op jit(solution)/shard_map/psum | solution.py:38
  540.5 96.9 %all-reduce.21.cloned.1.call-start = ((), (), s32[]{:S(2)}) async-start(), calls=%async_computation.28 | async-start | bytes 1572864 | tf_op jit(solution)/shard_map/psum | solution.py:38
  655.5 116.4 %reduce-scatter.83.cloned.1.call-start = ((), (), s32[]{:S(2)}) async-start(), calls=%async_computation.51 | async-start | bytes 294912
  656.6 151.8 %reduce-scatter.87.cloned.1.call-start = ((), (), s32[]{:S(2)}) async-start(), calls=%async_computation.53 | async-start | bytes 294912
  657.6 189.0 %reduce-scatter.71.cloned.1.call-start = ((), (), s32[]{:S(2)}) async-start(), calls=%async_computation.45 | async-start | bytes 589824
  659.0 223.8 %reduce-scatter.67.cloned.1.call-start = ((), (), s32[]{:S(2)}) async-start(), calls=%async_computation.43 | async-start | bytes 73728
  660.0 267.7 %reduce-scatter.79.cloned.1.call-start = ((), (), s32[]{:S(2)}) async-start(), calls=%async_computation.49 | async-start | bytes 2359296
  664.7 299.5 %reduce-scatter.73.cloned.1.call-start = ((), (), s32[]{:S(2)}) async-start(), calls=%async_computation.46 | async-start | bytes 294912
  666.2 335.0 %reduce-scatter.81.cloned.1.call-start = ((), (), s32[]{:S(2)}) async-start(), calls=%async_computation.50 | async-start | bytes 294912
  667.2 370.4 %reduce-scatter.85.cloned.1.call-start = ((), (), s32[]{:S(2)}) async-start(), calls=%async_computation.52 | async-start | bytes 294912
  668.2 411.4 %reduce-scatter.63.cloned.1.call-start = ((), (), s32[]{:S(2)}) async-start(), calls=%async_computation.41 | async-start | bytes 1769472
  675.2 442.6 %reduce-scatter.69.cloned.1.call-start = ((), (), s32[]{:S(2)}) async-start(), calls=%async_computation.44 | async-start | bytes 589824
  678.5 475.6 %reduce-scatter.65.cloned.1.call-start = ((), (), s32[]{:S(2)}) async-start(), calls=%async_computation.42 | async-start | bytes 73728
  683.2 515.6 %reduce-scatter.77.cloned.1.call-start = ((), (), s32[]{:S(2)}) async-start(), calls=%async_computation.48 | async-start | bytes 2359296
  690.4 552.9 %reduce-scatter.59.cloned.1.call-start = ((), (), s32[]{:S(2)}) async-start(), calls=%async_computation.33 | async-start | bytes 2359296 | tf_op jit(solution)/shard_map/reduce_scatter | solution.py:303
  693.8 594.4 %reduce-scatter.57.cloned.1.call-start = ((), (), s32[]{:S(2)}) async-start(), calls=%async_computation.32 | async-start | bytes 2359296 | tf_op jit(solution)/shard_map/reduce_scatter | solution.py:303
  696.2 638.6 %all-reduce.23.cloned.1.call-start = ((), (), s32[]{:S(2)}) async-start(), calls=%async_computation.31 | async-start | bytes 1572864 | tf_op jit(solution)/shard_map/psum | solution.py:38
  700.3 675.5 %reduce-scatter.61.cloned.1.call-start = ((), (), s32[]{:S(2)}) async-start(), calls=%async_computation.40 | async-start | bytes 1769472
  (117 other events, 1896.0 us)
Sparse Core Ops, SparseCore 0:
  61.4 43.6 all-reduce.8
  168.6 43.6 all-reduce.10
  267.3 43.7 all-reduce.12
  374.1 43.6 all-reduce.14
  428.2 42.9 all-reduce.16
  540.6 43.6 all-reduce.18
  594.4 42.9 all-reduce.20
  701.3 33.6 reduce-scatter.74
  738.2 33.5 reduce-scatter.82
  774.8 33.6 reduce-scatter.86
  812.4 34.1 reduce-scatter.70
  849.6 33.1 reduce-scatter.66
  886.4 41.2 reduce-scatter.78
  930.6 33.5 reduce-scatter.72
  967.5 33.6 reduce-scatter.80
  1004.0 33.5 reduce-scatter.84
  1041.2 38.4 reduce-scatter.62
  1083.6 34.0 reduce-scatter.68
  1120.8 33.2 reduce-scatter.64
  1157.5 41.2 reduce-scatter.76
  1202.1 41.2 reduce-scatter.58
  1247.0 41.2 reduce-scatter.56
  1291.1 43.6 all-reduce.22
  1338.0 37.7 reduce-scatter.60
  (10 shorter events, 256.1 us)
where the time goes:
time: 1400 us; the launch traced here: 1390 us
  waiting for transfers between devices  1040 us (74%)
  blocking collectives  120 us (9%)
  local copies, waits for them, and re-layouts  88.3 us (6%)
  matrix products  73 us (5%)
  other arithmetic  44.1 us (3%)
  between operations  16.3 us (1%)
    unnamed x48, waiting for transfers between devices  519 us
    psum x4, waiting for transfers between devices, tensor_back_sum(): return lax.psum(term, 'tp')  173 us
    psum x4, waiting for transfers between devices, tensor_sum(): return lax.psum(term, 'tp')  92 us
    reduce_scatter x2, waiting for transfers between devices, shards(): lax.psum_scatter(grad_terms[3].astype(jnp.bfloat16), ('shard', 'ctx'), sc...  87.3 us
    all_gather x2, waiting for transfers between devices, fetch_forward(): lax.all_gather(ff_in[layer_index], ('shard', 'ctx'), axis=0, tiled=True)  53.9 us
    unnamed x253, local copies, waits for them, and re-layouts  53.6 us
    all_gather x2, waiting for transfers between devices, fetch_forward(): lax.all_gather(ff_out[layer_index], ('shard', 'ctx'), axis=1, tiled=True)  51.2 us
  transfers between devices with their start and end apart: 34, of which 33 were waited for; matrix products, arithmetic and copies ran while one was open for 8% of the time, Pallas kernels for 0%

commit v1 on v0

v1 whole, which is shorter than its diff:
```python
import functools

import jax
import jax.numpy as jnp
from jax import lax
from jax.experimental import pallas as pl
from jax.experimental.pallas import tpu as pltpu
from jax.sharding import PartitionSpec as P

HD = 64
LANES = 128
SCORE_FLOOR = -1e30
PLANE = ("shard", "ctx")
BF = jnp.bfloat16
F32 = jnp.float32


def dot(left, right):
    return jnp.dot(left, right, preferred_element_type=F32)


def dot_nt(left, right):
    return lax.dot_general(left, right, (((1,), (1,)), ((), ())), preferred_element_type=F32)


def dot_tn(left, right):
    return lax.dot_general(left, right, (((0,), (0,)), ((), ())), preferred_element_type=F32)


def sds(shape, kind):
    return jax.ShapeDtypeStruct(shape, kind)


def whole():
    return pl.BlockSpec(memory_space=pltpu.VMEM)


def call(body, out_shape, in_specs, *operands, flops=0, name=None):
    moved = sum(o.size * o.dtype.itemsize for o in operands)
    moved += sum(o.size * o.dtype.itemsize for o in out_shape)
    return pl.pallas_call(
        body,
        out_shape=out_shape,
        in_specs=in_specs,
        out_specs=[whole() for _ in out_shape],
        compiler_params=pltpu.CompilerParams(vmem_limit_bytes=40 * 1024 * 1024),
        cost_estimate=pl.CostEstimate(flops=flops, bytes_accessed=moved, transcendentals=0),
        name=name,
    )(*operands)


def swap(value, axis, size, flip):
    return lax.ppermute(value, axis, [(i, i ^ flip) for i in range(size)])


def swap_all(pieces, axis, size):
    order = [k for k in (2, 3, 1) if k < size] + list(range(4, size))
    got = {k: swap(pieces[k], axis, size, k) for k in order}
    return [got[k] for k in range(1, size)]


def pick(blocks, index):
    return lax.dynamic_index_in_dim(blocks, index, 0, False)


def reorder(blocks, me):
    return jnp.stack([pick(blocks, me ^ k) for k in range(blocks.shape[0])])


def pack_in(matrix):
    c, rows, cols = matrix.shape
    return matrix.reshape(c, rows, cols // LANES, LANES).transpose(0, 2, 1, 3).reshape(-1, LANES)


def unpack_in(packed, c, rows, cols):
    return (
        packed.reshape(c, cols // LANES, rows, LANES).transpose(0, 2, 1, 3).reshape(c, rows, cols)
    )


def blocks_of_rows(matrix):
    c, depth, cols = matrix.shape
    cut = matrix.reshape(c, depth // LANES, LANES, cols // LANES, LANES)
    return cut.transpose(1, 0, 3, 2, 4).reshape(depth // LANES, -1, LANES)


def rows_of_blocks(packed, c, cols):
    blocks = packed.shape[0]
    cut = packed.reshape(blocks, c, cols // LANES, LANES, LANES)
    return cut.transpose(1, 0, 3, 2, 4).reshape(c, blocks * LANES, cols)


def blocks_of_cols(matrix):
    rows, width = matrix.shape
    return matrix.reshape(rows, width // LANES, LANES).transpose(1, 0, 2)


def cols_of_blocks(packed):
    blocks, rows, _ = packed.shape
    return packed.transpose(1, 0, 2).reshape(rows, blocks * LANES)


def gather_first(attn_in, smalls, shard_n, ctx_n, me, fast):
    if not fast:
        full = lax.all_gather(attn_in, PLANE, axis=1, tiled=True)
        rows = lax.all_gather(smalls, PLANE, axis=1, tiled=True)
        return blocks_of_rows(full), rows
    own = jnp.concatenate([pack_in(attn_in), smalls], axis=0)
    half = own.shape[0] // 2
    over_x = swap(own, "shard", 2, 1)
    over_y = swap(own, "ctx", 4, 2)
    across = jnp.concatenate(
        [swap(over_y[:half], "shard", 2, 1), swap(over_x[half:], "ctx", 4, 2)], axis=0
    )
    mine = jnp.stack([own, over_y, over_x, across])
    other = swap(mine, "ctx", 4, 1)
    both = jnp.stack([mine, other], axis=1).reshape(8, own.shape[0], LANES)
    natural = reorder(both, me)
    count = smalls.shape[0]
    small_rows = natural[:, -count:].transpose(1, 0, 2).reshape(count, -1)
    return natural[:, :-count], small_rows


def gather_in(attn_in, fast):
    if not fast:
        return blocks_of_rows(lax.all_gather(attn_in, PLANE, axis=1, tiled=True))
    return lax.all_gather(pack_in(attn_in), PLANE, axis=0, tiled=False)


def gather_rest(ff_in, ff_out, attn_out, fast):
    if not fast:
        up = lax.all_gather(ff_in, PLANE, axis=0, tiled=True)
        down = lax.all_gather(ff_out, PLANE, axis=1, tiled=True)
        out = lax.all_gather(attn_out, PLANE, axis=1, tiled=True)
        return jnp.concatenate(
            [blocks_of_rows(up[None]), blocks_of_cols(down), blocks_of_cols(out)], axis=1
        )
    own = jnp.concatenate([pack_in(ff_in[None]), ff_out, attn_out], axis=0)
    return lax.all_gather(own, PLANE, axis=0, tiled=False)


def scatter_ff(packed, hidden, fast):
    if not fast:
        up = rows_of_blocks(packed[:, :hidden], 1, hidden)[0]
        down = cols_of_blocks(packed[:, hidden:])
        return (
            lax.psum_scatter(up, PLANE, scatter_dimension=0, tiled=True).astype(F32),
            lax.psum_scatter(down, PLANE, scatter_dimension=1, tiled=True).astype(F32),
        )
    own = lax.psum_scatter(packed, PLANE, scatter_dimension=0, tiled=False)
    up = unpack_in(own[:hidden], 1, LANES, hidden)[0]
    return up.astype(F32), own[hidden:].astype(F32)


def scatter_attn(packed, width, fast):
    cut = packed.shape[1] - width
    if not fast:
        stack = rows_of_blocks(packed[:, :cut], 3, width)
        out = cols_of_blocks(packed[:, cut:])
        return (
            lax.psum_scatter(stack, PLANE, scatter_dimension=1, tiled=True).astype(F32),
            lax.psum_scatter(out, PLANE, scatter_dimension=1, tiled=True).astype(F32),
        )
    own = lax.psum_scatter(packed, PLANE, scatter_dimension=0, tiled=False)
    return unpack_in(own[:cut], 3, LANES, width).astype(F32), own[cut:].astype(F32)


def join(refs, target):
    step = refs[0].shape[0]
    for k, ref in enumerate(refs):
        target[k * step : (k + 1) * step, :] = ref[...]


def split_rows(value, refs, columns=slice(None)):
    step = refs[0].shape[0]
    for k, ref in enumerate(refs):
        ref[:, columns] = value[k * step : (k + 1) * step].astype(ref.dtype)


def in_matrix(w, c, halves):
    depth = w.shape[0] * LANES
    return jnp.concatenate(
        [
            w[:, (c * halves + h) * LANES : (c * halves + h + 1) * LANES, :].reshape(depth, LANES)
            for h in range(halves)
        ],
        axis=1,
    )


def up_pair(w, pair):
    depth = w.shape[0] * LANES
    return jnp.concatenate(
        [w[:, n * LANES : (n + 1) * LANES, :].reshape(depth, LANES) for n in (2 * pair, 2 * pair + 1)],
        axis=1,
    )


def down_pair(w, pair, first, count):
    return jnp.concatenate(
        [w[s, first : first + count, :] for s in (2 * pair, 2 * pair + 1)], axis=1
    )


def qkv_body(n, *refs):
    x_refs, (w, bias, x_out, q_out, kv_out) = refs[:n], refs[n:]
    join(x_refs, x_out)
    x = x_out[...]
    width = q_out.shape[1]
    halves = width // LANES
    q_out[...] = (dot(x, in_matrix(w, 0, halves)) + bias[0:1, :]).astype(BF)
    kv_out[:, :width] = dot(x, in_matrix(w, 1, halves)).astype(BF)
    kv_out[:, width:] = (dot(x, in_matrix(w, 2, halves)) + bias[1:2, :]).astype(BF)


def attend_body(m, n, *refs):
    q_ref, kv_refs = refs[0], refs[1 : 1 + m]
    seg_q, seg_k, w = refs[1 + m : 4 + m]
    o_out, lse_out, kv_all = refs[4 + m : 7 + m]
    pieces = refs[7 + m :]
    join(kv_refs, kv_all)
    width = q_ref.shape[1]
    same = seg_q[...] == seg_k[...]
    for h in range(width // HD):
        cols = slice(h * HD, (h + 1) * HD)
        vcols = slice(width + h * HD, width + (h + 1) * HD)
        s = dot_nt(q_ref[:, cols], kv_all[:, cols]) * HD ** (-0.5)
        s = jnp.where(same, s, SCORE_FLOOR)
        top = jnp.max(s, axis=-1, keepdims=True)
        e = jnp.exp(s - top)
        total = jnp.sum(e, axis=-1, keepdims=True)
        prob = (e / total).astype(BF)
        lse_out[:, h : h + 1] = top + jnp.log(total)
        o_out[:, cols] = dot(prob, kv_all[:, vcols]).astype(BF)
    o = o_out[...]
    for pair in range(w.shape[0] // 2):
        span = slice(2 * pair * LANES, (2 * pair + 2) * LANES)
        split_rows(dot(o, down_pair(w, pair, 0, width)), pieces, span)


def norm_body(n, *refs):
    base, own = refs[0], refs[1]
    others = refs[2 : 1 + n]
    shift, gain, centre_shift, out, out_low, normed, inverse = refs[1 + n :]
    r = base[...] + own[...]
    for other in others:
        r = r + other[...].astype(F32)
    r = r + shift[...]
    centre = r - jnp.mean(r, axis=-1, keepdims=True)
    inv = lax.rsqrt(jnp.mean(centre * centre, axis=-1, keepdims=True) + 1e-12)
    norm = centre * inv
    y = norm * gain[...] + centre_shift[...]
    out[...] = y
    out_low[...] = y.astype(BF)
    normed[...] = norm
    inverse[...] = jnp.broadcast_to(inv, inverse.shape)


def ff_body(n, *refs):
    h_refs = refs[:n]
    w, bias, h_out, slope_out, act_out = refs[n : n + 5]
    pieces = refs[n + 5 :]
    join(h_refs, h_out)
    h = h_out[...]
    hidden = act_out.shape[1]
    for pair in range(hidden // (2 * LANES)):
        span = slice(2 * pair * LANES, (2 * pair + 2) * LANES)
        u = dot(h, up_pair(w, pair)) + bias[:, span]
        cdf = 0.5 * (1.0 + lax.erf(u * (0.5**0.5)))
        act_out[:, span] = (u * cdf).astype(BF)
        slope_out[:, span] = cdf + u * (jnp.exp(-0.5 * u * u) * 0.3989422804014327)
    act = act_out[...]
    for pair in range(w.shape[0] // 2):
        span = slice(2 * pair * LANES, (2 * pair + 2) * LANES)
        split_rows(dot(act, down_pair(w, pair, hidden, hidden)), pieces, span)


def norm_back_body(n, *refs):
    base, own = refs[0], refs[1 : 2 if n else 1]
    others = refs[2 : 1 + n] if n else ()
    normed, inverse, gain, grad, grad_low, sums = refs[1 + n :]
    dy = base[...]
    for ref in own:
        dy = dy + ref[...]
    for ref in others:
        dy = dy + ref[...].astype(F32)
    norm = normed[...]
    e = dy * gain[...]
    dr = inverse[:, 0:1] * (
        e
        - jnp.mean(e, axis=-1, keepdims=True)
        - norm * jnp.mean(e * norm, axis=-1, keepdims=True)
    )
    grad[...] = dr
    grad_low[...] = dr.astype(BF)
    sums[...] = jnp.zeros_like(sums)
    sums[0:1, :] = jnp.sum(dy * norm, axis=0, keepdims=True)
    sums[1:2, :] = jnp.sum(dy, axis=0, keepdims=True)
    sums[2:3, :] = jnp.sum(dr, axis=0, keepdims=True)


def ff_back_body(n, *refs):
    g_refs = refs[:n]
    w, slope, g_out, du_out, bias_out = refs[n : n + 5]
    pieces = refs[n + 5 : 2 * n + 5]
    total = refs[2 * n + 5]
    join(g_refs, g_out)
    hidden = du_out.shape[1]
    for pair in range(w.shape[0] // 2):
        span = slice(2 * pair * LANES, (2 * pair + 2) * LANES)
        term = dot_nt(g_out[:, span], down_pair(w, pair, hidden, hidden))
        total[...] = term if pair == 0 else total[...] + term
    du = (total[...] * slope[...]).astype(BF)
    du_out[...] = du
    bias_out[...] = jnp.broadcast_to(
        jnp.sum(du.astype(F32), axis=0, keepdims=True), bias_out.shape
    )
    for pair in range(hidden // (2 * LANES)):
        span = slice(2 * pair * LANES, (2 * pair + 2) * LANES)
        term = dot_nt(du_out[:, span], up_pair(w, pair))
        total[...] = term if pair == 0 else total[...] + term
    split_rows(total[...], pieces)


def ff_grad_body(h_ref, act_ref, g_ref, du_ref, out):
    h, act = h_ref[...], act_ref[...]
    hidden = act.shape[1]
    blocks = out.shape[0]
    for pair in range(hidden // (2 * LANES)):
        span = slice(2 * pair * LANES, (2 * pair + 2) * LANES)
        grad = dot_tn(h, du_ref[:, span]).astype(BF).reshape(blocks, LANES, 2 * LANES)
        for j in range(2):
            n = 2 * pair + j
            out[:, n * LANES : (n + 1) * LANES, :] = grad[:, :, j * LANES : (j + 1) * LANES]
    for pair in range(blocks // 2):
        span = slice(2 * pair * LANES, (2 * pair + 2) * LANES)
        grad = dot_tn(act, g_ref[:, span]).astype(BF)
        for j in range(2):
            out[2 * pair + j, hidden : 2 * hidden, :] = grad[:, j * LANES : (j + 1) * LANES]


def attend_back_body(n, m, *refs):
    g_refs = refs[:n]
    w, q_ref, kv, lse, seg_q, seg_k, g_out, dq_out, near_out, far_out, do_ref, grads = refs[n:]
    join(g_refs, g_out)
    width = q_ref.shape[1]
    scale = HD ** (-0.5)
    for pair in range(w.shape[0] // 2):
        span = slice(2 * pair * LANES, (2 * pair + 2) * LANES)
        term = dot_nt(g_out[:, span], down_pair(w, pair, 0, width))
        total = term if pair == 0 else total + term
    do_ref[...] = total.astype(BF)
    same = seg_q[...] == seg_k[...]
    for h in range(width // HD):
        cols = slice(h * HD, (h + 1) * HD)
        vcols = slice(width + h * HD, width + (h + 1) * HD)
        s = dot_nt(q_ref[:, cols], kv[:, cols]) * scale
        s = jnp.where(same, s, SCORE_FLOOR)
        prob = jnp.exp(s - lse[:, h : h + 1])
        dp = dot_nt(do_ref[:, cols], kv[:, vcols])
        row = jnp.sum(dp * prob, axis=-1, keepdims=True)
        ds = (prob * (dp - row)).astype(BF)
        dq_out[:, cols] = (dot(ds, kv[:, cols]) * scale).astype(BF)
        grads[:, cols] = dot_tn(ds, q_ref[:, cols]) * scale
        grads[:, vcols] = dot_tn(prob.astype(BF), do_ref[:, cols])
    step = q_ref.shape[0]
    for j in range(m // 2):
        near_out[j] = grads[2 * j * step : (2 * j + 1) * step, :]
        far_out[j] = grads[(2 * j + 1) * step : (2 * j + 2) * step, :].astype(BF)


def qkv_back_body(n, near, got, last, dq, w, kv_out, *pieces):
    width = dq.shape[1]
    halves = width // LANES
    kv_out[...] = (near[0] + got[0].astype(F32) + last[...].astype(F32)).astype(BF)
    total = dot_nt(dq[...], in_matrix(w, 0, halves))
    total = total + dot_nt(kv_out[:, :width], in_matrix(w, 1, halves))
    total = total + dot_nt(kv_out[:, width:], in_matrix(w, 2, halves))
    split_rows(total, pieces)


def attn_grad_body(x_ref, dq, dkv, o_ref, g_ref, out, sums):
    x = x_ref[...]
    width = dq.shape[1]
    halves = width // LANES
    blocks = out.shape[0]
    for c in range(3):
        d = dq[...] if c == 0 else dkv[:, (c - 1) * width : c * width]
        grad = dot_tn(x, d).astype(BF).reshape(blocks, LANES, width)
        for h in range(halves):
            first = (c * halves + h) * LANES
            out[:, first : first + LANES, :] = grad[:, :, h * LANES : (h + 1) * LANES]
    first = 3 * width
    o = o_ref[...]
    for pair in range(blocks // 2):
        span = slice(2 * pair * LANES, (2 * pair + 2) * LANES)
        grad = dot_tn(o, g_ref[:, span]).astype(BF)
        for j in range(2):
            out[2 * pair + j, first : first + width, :] = grad[:, j * LANES : (j + 1) * LANES]
    sums[...] = jnp.zeros_like(sums)
    sums[0:1, :] = jnp.sum(dq[...].astype(F32), axis=0, keepdims=True)
    sums[1:2, :] = jnp.sum(dkv[:, width:].astype(F32), axis=0, keepdims=True)


def shards(sizes, *args):
    shard_n, ctx_n, tp_n = sizes
    (
        hidden_in,
        seg_ids,
        attn_in,
        attn_bias,
        attn_out,
        ff_in,
        ff_bias,
        ff_out,
        gains,
        shifts,
        cotangent,
    ) = args
    packs, tok, depth = hidden_in.shape
    layers = attn_in.shape[0]
    width = attn_in.shape[3]
    hidden = ff_in.shape[2]
    plane_n = shard_n * ctx_n
    blocks = depth // LANES
    fast = (shard_n, ctx_n) == (2, 4) and blocks == 8
    step = tok // tp_n
    tp_me = lax.axis_index("tp")
    ctx_me = lax.axis_index("ctx")
    me = lax.axis_index("shard") * ctx_n + ctx_me
    share = depth // plane_n

    smalls = jnp.concatenate(
        [
            gains.reshape(2 * layers, share),
            shifts.reshape(4 * layers, share),
            ff_bias.reshape(layers, -1),
            attn_bias.reshape(-1, share),
        ],
        axis=0,
    )
    used = smalls.shape[0]
    smalls = jnp.pad(smalls, ((0, -used % 16), (0, 0)))

    first_in, rows = gather_first(attn_in[0], smalls, shard_n, ctx_n, me, fast)
    rest = [gather_rest(ff_in[l], ff_out[l], attn_out[l], fast) for l in range(layers)]
    stacks = [first_in] + [gather_in(attn_in[l], fast) for l in range(1, layers)]

    rows_f = rows.astype(F32)
    at = 6 * layers
    gain_row = lambda l, j: rows_f[2 * l + j][None]
    shift_row = lambda l, j: rows_f[2 * layers + 4 * l + j][None]
    up_bias = lambda l: rows_f[at + l][None]
    qv_bias = (
        rows_f[at + layers : used]
        .reshape(-1, plane_n, share)
        .transpose(1, 0, 2)
        .reshape(plane_n, layers, 2, width // plane_n)
        .transpose(1, 2, 0, 3)
        .reshape(layers, 2, width)
    )

    x_pieces = reorder(hidden_in.reshape(tp_n, step, depth), tp_me)
    seg_cut = reorder(seg_ids.reshape(ctx_n, tp_n, step), ctx_me)
    seg_cut = reorder(seg_cut.transpose(1, 0, 2), tp_me).transpose(1, 0, 2)
    seg_k = seg_cut.reshape(1, -1)
    seg_q = seg_cut[0].reshape(tok, 1)
    keys = ctx_n * tok
    heads = width // HD

    def piece_shapes():
        return [sds((step, depth), F32)] + [sds((step, depth), BF)] * (tp_n - 1)

    ff_w = [r[:, : 2 * hidden] for r in rest]
    out_w = [r[:, 2 * hidden :] for r in rest]
    matmul = lambda *dims: 2 * functools.reduce(lambda a, b: a * b, dims)

    base = x_pieces[0].astype(F32)
    low = [x_pieces[k] for k in range(tp_n)]
    kept = []
    for l in range(layers):
        x, q, kv = call(
            functools.partial(qkv_body, tp_n),
            [sds((tok, depth), BF), sds((tok, width), BF), sds((tok, 2 * width), BF)],
            [whole()] * (tp_n + 2),
            *low,
            stacks[l],
            qv_bias[l],
            flops=matmul(tok, depth, 3 * width),
            name="project_in",
        )
        over_y = swap(kv, "ctx", ctx_n, 2)
        over_core = swap(kv, "ctx", ctx_n, 1)
        over_both = swap(over_y, "ctx", ctx_n, 1)
        o, lse, kv_all, *a_pieces = call(
            functools.partial(attend_body, ctx_n, tp_n),
            [sds((tok, width), BF), sds((tok, heads), F32), sds((keys, 2 * width), BF)]
            + piece_shapes(),
            [whole()] * (ctx_n + 4),
            q,
            kv,
            over_core,
            over_y,
            over_both,
            seg_q,
            seg_k,
            out_w[l],
            flops=matmul(tok, keys, 2 * width) + matmul(tok, width, depth),
            name="attend",
        )
        got = swap_all(a_pieces, "tp", tp_n)

        def norm(base, own, got, shift, gain, move):
            return call(
                functools.partial(norm_body, tp_n),
                [
                    sds((step, depth), F32),
                    sds((step, depth), BF),
                    sds((step, depth), F32),
                    sds((step, LANES), F32),
                ],
                [whole()] * (tp_n + 4),
                base,
                own,
                *got,
                shift,
                gain,
                move,
                name="norm",
            )

        hid, hid_low, n1, inv1 = norm(
            base, a_pieces[0], got, shift_row(l, 0), gain_row(l, 0), shift_row(l, 1)
        )
        h_got = swap_all([hid_low] * tp_n, "tp", tp_n)
        h, slope, act, *f_pieces = call(
            functools.partial(ff_body, tp_n),
            [sds((tok, depth), BF), sds((tok, hidden), F32), sds((tok, hidden), BF)]
            + piece_shapes(),
            [whole()] * (tp_n + 2),
            hid_low,
            *h_got,
            ff_w[l],
            up_bias(l),
            flops=2 * matmul(tok, depth, hidden),
            name="feed_forward",
        )
        got = swap_all(f_pieces, "tp", tp_n)
        base, y_low, n2, inv2 = norm(
            hid, f_pieces[0], got, shift_row(l, 2), gain_row(l, 1), shift_row(l, 3)
        )
        low = [y_low] + swap_all([y_low] * tp_n, "tp", tp_n)
        kept.append((x, q, kv_all, lse, o, n1, inv1, h, slope, act, n2, inv2))
    hidden_out = reorder(jnp.stack(low), tp_me).reshape(packs, tok, depth)

    def norm_back(base, pieces, normed, inverse, gain):
        return call(
            functools.partial(norm_back_body, len(pieces)),
            [sds((step, depth), F32), sds((step, depth), BF), sds((8, depth), F32)],
            [whole()] * (4 + len(pieces)),
            base,
            *pieces,
            normed,
            inverse,
            gain,
            name="norm_back",
        )

    grad = pick(cotangent.reshape(tp_n, step, depth), tp_me).astype(F32)
    terms = []
    row_sums = [None] * layers
    ff_grads = [None] * layers
    attn_grads = [None] * layers
    for l in reversed(range(layers)):
        x, q, kv_all, lse, o, n1, inv1, h, slope, act, n2, inv2 = kept[l]
        dr2, df_low, sums2 = norm_back(grad, terms, n2, inv2, gain_row(l, 1))
        got = swap_all([df_low] * tp_n, "tp", tp_n)
        df, du, sums_up, *h_pieces = pl.pallas_call(
            functools.partial(ff_back_body, tp_n),
            out_shape=[sds((tok, depth), BF), sds((tok, hidden), BF), sds((8, hidden), F32)]
            + piece_shapes(),
            in_specs=[whole()] * (tp_n + 2),
            out_specs=[whole()] * (3 + tp_n),
            scratch_shapes=[pltpu.VMEM((tok, hidden), F32)],
            compiler_params=pltpu.CompilerParams(vmem_limit_bytes=40 * 1024 * 1024),
            cost_estimate=pl.CostEstimate(
                flops=2 * matmul(tok, depth, hidden),
                bytes_accessed=10 * 1024 * 1024,
                transcendentals=0,
            ),
            name="feed_forward_back",
        )(df_low, *got, ff_w[l], slope)
        got = swap_all(h_pieces, "tp", tp_n)
        (packed,) = call(
            ff_grad_body,
            [sds((blocks, 2 * hidden, LANES), BF)],
            [whole()] * 4,
            h,
            act,
            df,
            du,
            flops=2 * matmul(tok, depth, hidden),
            name="feed_forward_grad",
        )
        ff_grads[l] = scatter_ff(packed, hidden, fast)
        dr1, da_low, sums1 = norm_back(dr2, [h_pieces[0], *got], n1, inv1, gain_row(l, 0))
        got = swap_all([da_low] * tp_n, "tp", tp_n)
        da, dq, near, far = pl.pallas_call(
            functools.partial(attend_back_body, tp_n, ctx_n),
            out_shape=[
                sds((tok, depth), BF),
                sds((tok, width), BF),
                sds((ctx_n // 2, tok, 2 * width), F32),
                sds((ctx_n // 2, tok, 2 * width), BF),
            ],
            in_specs=[whole()] * (tp_n + 6),
            out_specs=[whole()] * 4,
            scratch_shapes=[pltpu.VMEM((tok, width), BF), pltpu.VMEM((keys, 2 * width), F32)],
            compiler_params=pltpu.CompilerParams(vmem_limit_bytes=40 * 1024 * 1024),
            cost_estimate=pl.CostEstimate(
                flops=5 * matmul(tok, keys, width) + matmul(tok, width, depth),
                bytes_accessed=8 * 1024 * 1024,
                transcendentals=0,
            ),
            name="attend_back",
        )(da_low, *got, out_w[l], q, kv_all, lse, seg_q, seg_k)
        got = swap(far, "ctx", ctx_n, 1)
        passed = (near[1] + got[1].astype(F32)).astype(BF)
        last = swap(passed, "ctx", ctx_n, 2)
        dkv, *x_pieces = call(
            functools.partial(qkv_back_body, tp_n),
            [sds((tok, 2 * width), BF)] + piece_shapes(),
            [whole()] * 5,
            near,
            got,
            last,
            dq,
            stacks[l],
            flops=matmul(tok, depth, 3 * width),
            name="project_in_back",
        )
        packed, sums_qv = call(
            attn_grad_body,
            [sds((blocks, 4 * width, LANES), BF), sds((8, width), F32)],
            [whole()] * 5,
            x,
            dq,
            dkv,
            o,
            da,
            flops=matmul(tok, depth, 4 * width),
            name="attend_grad",
        )
        attn_grads[l] = scatter_attn(packed, width, fast)
        grad = dr1
        terms = [x_pieces[0], *swap_all(x_pieces, "tp", tp_n)]
        row_sums[l] = (sums1, sums2, sums_up, sums_qv)

    total = grad + terms[0]
    for term in terms[1:]:
        total = total + term.astype(F32)
    total = total.astype(BF)
    pieces = [total] + swap_all([total] * tp_n, "tp", tp_n)
    grad_in = reorder(jnp.stack(pieces), tp_me).astype(F32).reshape(packs, tok, depth)

    small = []
    for sums1, sums2, _, _ in row_sums:
        small += [sums1[0:1], sums2[0:1]]
    for sums1, sums2, _, _ in row_sums:
        small += [sums1[2:3], sums1[1:2], sums2[2:3], sums2[1:2]]
    for _, _, sums_up, _ in row_sums:
        small += [sums_up[0:1]]
    qv = jnp.stack([s[3][0:2] for s in row_sums])
    qv = qv.reshape(layers, 2, plane_n, width // plane_n).transpose(2, 0, 1, 3)
    lines = jnp.concatenate(small, axis=0).reshape(-1, plane_n, share).transpose(1, 0, 2)
    lines = jnp.concatenate([lines, qv.reshape(plane_n, -1, share)], axis=1)
    lines = lax.all_to_all(lines, PLANE, 0, 0, tiled=True)
    lines = jnp.sum(lines, axis=0)
    norms = lines[: 6 * layers]
    flip = 1
    while flip < tp_n:
        norms = norms + swap(norms, "tp", tp_n, flip)
        flip *= 2
    grad_gains = norms[: 2 * layers].reshape(layers, 2, share)
    grad_shifts = norms[2 * layers :].reshape(layers, 4, share)
    grad_ff_bias = lines[6 * layers : 7 * layers].reshape(ff_bias.shape)
    grad_attn_bias = lines[7 * layers :].reshape(attn_bias.shape)

    return (
        hidden_out,
        grad_in,
        jnp.stack([g[0] for g in attn_grads]),
        grad_attn_bias,
        jnp.stack([g[1] for g in attn_grads]),
        jnp.stack([g[0] for g in ff_grads]),
        grad_ff_bias,
        jnp.stack([g[1] for g in ff_grads]),
        grad_gains,
        grad_shifts,
    )


def solution(mesh):
    in_specs = (
        P("shard", "ctx", None),
        P("shard", None),
        P(None, None, ("shard", "ctx"), "tp"),
        P(None, None, "tp", ("shard", "ctx")),
        P(None, "tp", ("shard", "ctx")),
        P(None, ("shard", "ctx"), "tp"),
        P(None, "tp", ("shard", "ctx")),
        P(None, "tp", ("shard", "ctx")),
        P(None, None, ("shard", "ctx")),
        P(None, None, ("shard", "ctx")),
        P("shard", "ctx", None),
    )
    out_specs = (
        P("shard", "ctx", None),
        P("shard", "ctx", None),
        P(None, None, ("shard", "ctx"), "tp"),
        P(None, None, "tp", ("shard", "ctx")),
        P(None, "tp", ("shard", "ctx")),
        P(None, ("shard", "ctx"), "tp"),
        P(None, "tp", ("shard", "ctx")),
        P(None, "tp", ("shard", "ctx")),
        P(None, None, ("shard", "ctx")),
        P(None, None, ("shard", "ctx")),
    )
    sizes = (mesh.shape["shard"], mesh.shape["ctx"], mesh.shape["tp"])
    return jax.shard_map(
        functools.partial(shards, sizes),
        mesh=mesh,
        in_specs=in_specs,
        out_specs=out_specs,
        check_vma=False,
    )
```

time: 1400 us -> 449 us (0.32)
  waiting for transfers between devices: 1040 us -> 236 us
  blocking collectives: 120 us -> 7.7 us
  starting transfers between devices: 2.04 us -> 88.2 us
  matrix products: 73 us -> 0 us
  other arithmetic: 44.1 us -> 11.1 us
  Pallas kernels: 0 us -> 30.7 us
  local copies, waits for them, and re-layouts: 88.3 us -> 58.1 us
    unnamed x48 -> x7, waiting for transfers between devices: 519 us -> 0.11 us
    psum x8 -> x0, waiting for transfers between devices: 265 us -> none  [the longest x4 173 us: tensor_back_sum(): return lax.psum(term, 'tp')]
    ppermute x0 -> x68, waiting for transfers between devices: none -> 133 us  [swap(): return lax.ppermute(value, axis, [(i, i ^ flip) for i in range(size)])]
    all_gather x6 -> x3, waiting for transfers between devices: 132 us -> 10.7 us  [the longest x2 10.7 us: gather_rest(): return lax.all_gather(own, PLANE, axis=0, tiled=False)]
    all_gather x14 -> x0, blocking collectives: 120 us -> none  [the longest x2 22.6 us: fetch_forward(): lax.all_gather(attn_out[layer_index], ('shard', 'ctx'), axis=1, tiled=True)]
    ppermute x0 -> x68, starting transfers between devices: none -> 87.9 us  [swap(): return lax.ppermute(value, axis, [(i, i ^ flip) for i in range(size)])]
    dot_general x36 -> x0, matrix products: 73 us -> none  [the longest x2 9.49 us: forward_layer(): jnp.dot(hidden_low, w_up, preferred_element_type=jnp.float32)]
    reduce_scatter x6 -> x4, waiting for transfers between devices: 125 us -> 92.4 us  [the longest x2 92.4 us: scatter_ff(): own = lax.psum_scatter(packed, PLANE, scatter_dimension=0, tiled=False)]
  transfers between devices with their start and end apart: 34 -> 75, of which waited for: 33 -> 45; matrix products, arithmetic and copies ran while one was open for 8% -> 7% of each run, Pallas kernels for 0% -> 4%
where the time goes in v1:
time: 449 us; the launch traced here: 447 us
  waiting for transfers between devices  236 us (53%)
  starting transfers between devices  88.2 us (20%)
  local copies, waits for them, and re-layouts  58.1 us (13%)
  Pallas kernels  30.7 us (7%)
  between operations  15.5 us (3%)
  other arithmetic  11.1 us (2%)
  blocking collectives  7.7 us (2%)
    ppermute x68, waiting for transfers between devices, swap(): return lax.ppermute(value, axis, [(i, i ^ flip) for i in range(size)])  133 us
    reduce_scatter x2, waiting for transfers between devices, scatter_ff(): own = lax.psum_scatter(packed, PLANE, scatter_dimension=0, tiled=False)  92.4 us
    ppermute x68, starting transfers between devices, swap(): return lax.ppermute(value, axis, [(i, i ^ flip) for i in range(size)])  87.9 us
    unnamed x153, local copies, waits for them, and re-layouts  32.2 us
    pallas_call x20, Pallas kernels, call(): pl.pallas_call(body, out_shape=out_shape, in_specs=in_specs, out_specs=[w...  20.4 us
    all_gather x2, waiting for transfers between devices, gather_rest(): return lax.all_gather(own, PLANE, axis=0, tiled=False)  10.7 us
  transfers between devices with their start and end apart: 75, of which 45 were waited for; matrix products, arithmetic and copies ran while one was open for 7% of the time, Pallas kernels for 4%

profile of v1, /device:TPU:0, one launch (start us, length us, event | category | flops | bytes accessed | tf_op | source)
XLA Modules:
  0.0 447.3 jit_solution(16024905535547916137)
XLA Ops:
  17.0 3.5 collective-permute-done
  38.0 9.5 %collective-permute-done.6.refs_3_ = bf16[192,512]{1,0:T(8,128)(2,1)S(1)} collective-permute-done((bf16[192,512]{1,0:T(8,128)(2,1)S(1)}, bf16[192,512]{1,0:T(8,128)(2,1)S(1)}, u32[]{:S(2)}, u32[]{:S(2)}) %collective-permute-start.6) | collective-permute-done | bytes 196640 | tf_op jit(solution)/shard_map/ppermute | solution.py:53
  47.8 9.9 %all-gather.8.cloned.1.call-done = bf16[18432,128]{1,0:T(8,128)(2,1)} async-done(((bf16[2304,128]{1,0:T(8,128)(2,1)}), bf16[18432,128]{1,0:T(8,128)(2,1)}) %all-gather.8.cloned.1.call-update) | async-done | bytes 4718608 | tf_op jit(solution)/shard_map/all_gather | solution.py:139
  70.4 7.3 %collective-permute-done.9.refs_3_ = bf16[48,1024]{1,0:T(8,128)(2,1)S(1)} collective-permute-done((bf16[48,1024]{1,0:T(8,128)(2,1)S(1)}, bf16[48,1024]{1,0:T(8,128)(2,1)S(1)}, u32[]{:S(2)}, u32[]{:S(2)}) %collective-permute-start.9) | collective-permute-done | bytes 98336 | tf_op jit(solution)/shard_map/ppermute | solution.py:53
  85.6 3.8 collective-permute-done.12.refs_2_
  98.3 5.1 %collective-permute-done.15.refs_3_ = bf16[48,1024]{1,0:T(8,128)(2,1)S(1)} collective-permute-done((bf16[48,1024]{1,0:T(8,128)(2,1)S(1)}, bf16[48,1024]{1,0:T(8,128)(2,1)S(1)}, u32[]{:S(2)}, u32[]{:S(2)}) %collective-permute-start.15) | collective-permute-done | bytes 98336 | tf_op jit(solution)/shard_map/ppermute | solution.py:53
  122.3 7.9 %collective-permute-done.21.refs_3_ = bf16[192,512]{1,0:T(8,128)(2,1)} collective-permute-done((bf16[192,512]{1,0:T(8,128)(2,1)}, bf16[192,512]{1,0:T(8,128)(2,1)}, u32[]{:S(2)}, u32[]{:S(2)}) %collective-permute-start.21) | collective-permute-done | bytes 196640 | tf_op jit(solution)/shard_map/ppermute | solution.py:53
  132.1 3.6 attend.3
  141.4 7.5 %collective-permute-done.24.refs_3_ = bf16[48,1024]{1,0:T(8,128)(2,1)S(1)} collective-permute-done((bf16[48,1024]{1,0:T(8,128)(2,1)S(1)}, bf16[48,1024]{1,0:T(8,128)(2,1)S(1)}, u32[]{:S(2)}, u32[]{:S(2)}) %collective-permute-start.24) | collective-permute-done | bytes 98336 | tf_op jit(solution)/shard_map/ppermute | solution.py:53
  157.5 3.6 collective-permute-done.27.refs_2_
  169.6 5.0 %collective-permute-done.30.refs_3_ = bf16[48,1024]{1,0:T(8,128)(2,1)S(1)} collective-permute-done((bf16[48,1024]{1,0:T(8,128)(2,1)S(1)}, bf16[48,1024]{1,0:T(8,128)(2,1)S(1)}, u32[]{:S(2)}, u32[]{:S(2)}) %collective-permute-start.30) | collective-permute-done | bytes 98336 | tf_op jit(solution)/shard_map/ppermute | solution.py:53
  193.0 4.5 %collective-permute-done.39.refs_3_ = bf16[48,1024]{1,0:T(8,128)(2,1)S(1)} collective-permute-done((bf16[48,1024]{1,0:T(8,128)(2,1)S(1)}, bf16[48,1024]{1,0:T(8,128)(2,1)S(1)}, u32[]{:S(2)}, u32[]{:S(2)}) %collective-permute-start.39) | collective-permute-done | bytes 98336 | tf_op jit(solution)/shard_map/ppermute | solution.py:53
  207.5 3.7 attend_back.2
  213.1 6.9 %collective-permute-done.45.last = bf16[192,512]{1,0:T(8,128)(2,1)S(1)} collective-permute-done((bf16[192,512]{1,0:T(8,128)(2,1)S(1)}, bf16[192,512]{1,0:T(8,128)(2,1)S(1)}, u32[]{:S(2)}, u32[]{:S(2)}) %collective-permute-start.45) | collective-permute-done | bytes 196640 | tf_op jit(solution)/shard_map/ppermute | solution.py:53
  229.2 5.1 %collective-permute-done.47.refs_3_ = bf16[48,1024]{1,0:T(8,128)(2,1)S(1)} collective-permute-done((bf16[48,1024]{1,0:T(8,128)(2,1)}, bf16[48,1024]{1,0:T(8,128)(2,1)S(1)}, u32[]{:S(2)}, u32[]{:S(2)}) %collective-permute-start.47) | collective-permute-done | bytes 98336 | tf_op jit(solution)/shard_map/ppermute | solution.py:53
  256.7 4.8 %collective-permute-done.53.refs_3_ = bf16[48,1024]{1,0:T(8,128)(2,1)S(1)} collective-permute-done((bf16[48,1024]{1,0:T(8,128)(2,1)S(1)}, bf16[48,1024]{1,0:T(8,128)(2,1)S(1)}, u32[]{:S(2)}, u32[]{:S(2)}) %collective-permute-start.53) | collective-permute-done | bytes 98336 | tf_op jit(solution)/shard_map/ppermute | solution.py:53
  268.4 3.2 collective-permute-done.56.refs_2_
  271.5 3.6 attend_back.3
  277.2 6.9 %collective-permute-done.59.last = bf16[192,512]{1,0:T(8,128)(2,1)S(1)} collective-permute-done((bf16[192,512]{1,0:T(8,128)(2,1)S(1)}, bf16[192,512]{1,0:T(8,128)(2,1)S(1)}, u32[]{:S(2)}, u32[]{:S(2)}) %collective-permute-start.59) | collective-permute-done | bytes 196640 | tf_op jit(solution)/shard_map/ppermute | solution.py:53
  305.1 7.7 %all_to_all.5 = f32[8,15,128]{2,1,0:T(8,128)S(1)} all-to-all(f32[8,15,128]{2,1,0:T(8,128)S(1)} %pad_maximum_fusion.9), channel_id=1, replica_groups=mesh['shard'=2,'ctx'=4,'tp'=4] {'shard','ctx'}, dimensions={0} | all-to-all | bytes 122880 | tf_op jit(solution)/shard_map/all_to_all | solution.py:677
  318.7 6.2 %collective-permute-done.61 = bf16[48,1024]{1,0:T(8,128)(2,1)S(1)} collective-permute-done((bf16[48,1024]{1,0:T(8,128)(2,1)S(1)}, bf16[48,1024]{1,0:T(8,128)(2,1)S(1)}, u32[]{:S(2)}, u32[]{:S(2)}) %collective-permute-start.61) | collective-permute-done | bytes 98336 | tf_op jit(solution)/shard_map/ppermute | solution.py:53
  332.5 4.0 collective-permute-done.64
  343.7 38.4 %reduce-scatter.11.cloned.1.call-done = bf16[1,2048,128]{2,1,0:T(8,128)(2,1)} async-done(((bf16[8,2048,128]{2,1,0:T(8,128)(2,1)}), bf16[1,2048,128]{2,1,0:T(8,128)(2,1)}) %reduce-scatter.11.cloned.1.call-update) | async-done | bytes 524304 | tf_op jit(solution)/shard_map/reduce_scatter | solution.py:150
  383.2 54.0 %reduce-scatter.9.cloned.1.call-done = bf16[1,2048,128]{2,1,0:T(8,128)(2,1)} async-done(((bf16[8,2048,128]{2,1,0:T(8,128)(2,1)}), bf16[1,2048,128]{2,1,0:T(8,128)(2,1)}) %reduce-scatter.9.cloned.1.call-update) | async-done | bytes 524304 | tf_op jit(solution)/shard_map/reduce_scatter | solution.py:150
  (407 shorter events, 216.2 us)
Async XLA Ops:
  7.2 50.5 %all-gather.8.cloned.1.call-start = ((), (), s32[]{:S(2)}) async-start(), calls=%async_computation.10 | async-start | bytes 5308416 | tf_op jit(solution)/shard_map/all_gather | solution.py:139
  10.2 101.1 %all-gather.6.cloned.1.call-start = ((), (), s32[]{:S(2)}) async-start(), calls=%async_computation.5 | async-start | bytes 1769472 | tf_op jit(solution)/shard_map/all_gather | solution.py:127
  11.1 119.8 %all-gather.10.cloned.1.call-start = ((), (), s32[]{:S(2)}) async-start(), calls=%async_computation.11 | async-start | bytes 5308416 | tf_op jit(solution)/shard_map/all_gather | solution.py:139
  12.1 326.4 %reduce-scatter.7.cloned.1.call-start = ((), (), s32[]{:S(2)}) async-start(), calls=%async_computation.7 | async-start | bytes 2359296 | tf_op jit(solution)/shard_map/reduce_scatter | solution.py:164
  36.4 11.1 %collective-permute-start.6 = (bf16[192,512]{1,0:T(8,128)(2,1)S(1)}, bf16[192,512]{1,0:T(8,128)(2,1)S(1)}, u32[]{:S(2)}, u32[]{:S(2)}) collective-permute-start(bf16[192,512]{1,0:T(8,128)(2,1)S(1)} %get-tuple-element.108.refs_1_), channel_id=1, source_target_pairs={{0,8},{4,12},{8,0},{12,4},{1,9},{5,13},{9,1},{13,5},{2,10},{6,14},... | collective-permute-start | bytes 589832 | tf_op jit(solution)/shard_map/ppermute | solution.py:53
  37.9 20.9 %collective-permute-start.5 = (bf16[192,512]{1,0:T(8,128)(2,1)S(1)}, bf16[192,512]{1,0:T(8,128)(2,1)S(1)}, u32[]{:S(2)}, u32[]{:S(2)}) collective-permute-start(bf16[192,512]{1,0:T(8,128)(2,1)S(1)} %get-tuple-element.108.refs_1_), channel_id=1, source_target_pairs={{0,4},{4,0},{8,12},{12,8},{1,5},{5,1},{9,13},{13,9},{2,6},{6,2},{1... | collective-permute-start | bytes 589832 | tf_op jit(solution)/shard_map/ppermute | solution.py:53
  47.5 12.0 %collective-permute-start.7 = (bf16[192,512]{1,0:T(8,128)(2,1)S(1)}, bf16[192,512]{1,0:T(8,128)(2,1)S(1)}, u32[]{:S(2)}, u32[]{:S(2)}) collective-permute-start(bf16[192,512]{1,0:T(8,128)(2,1)S(1)} %collective-permute-done.6.refs_3_), channel_id=1, source_target_pairs={{0,4},{4,0},{8,12},{12,8},{1,5},{5,1},{9,13},{13,9},{2,6},{6,2},{1... | collective-permute-start | bytes 589832 | tf_op jit(solution)/shard_map/ppermute | solution.py:53
  67.1 10.6 %collective-permute-start.9 = (bf16[48,1024]{1,0:T(8,128)(2,1)S(1)}, bf16[48,1024]{1,0:T(8,128)(2,1)S(1)}, u32[]{:S(2)}, u32[]{:S(2)}) collective-permute-start(bf16[48,1024]{1,0:T(8,128)(2,1)S(1)} %get-tuple-element.111), channel_id=1, source_target_pairs={{0,2},{1,3},{2,0},{3,1},{4,6},{5,7},{6,4},{7,5},{8,10},{9,11},{10,... | collective-permute-start | bytes 294920 | tf_op jit(solution)/shard_map/ppermute | solution.py:53
  93.0 10.4 %collective-permute-start.15 = (bf16[48,1024]{1,0:T(8,128)(2,1)S(1)}, bf16[48,1024]{1,0:T(8,128)(2,1)S(1)}, u32[]{:S(2)}, u32[]{:S(2)}) collective-permute-start(bf16[48,1024]{1,0:T(8,128)(2,1)S(1)} %get-tuple-element.117), channel_id=1, source_target_pairs={{0,2},{1,3},{2,0},{3,1},{4,6},{5,7},{6,4},{7,5},{8,10},{9,11},{10,... | collective-permute-start | bytes 294920 | tf_op jit(solution)/shard_map/ppermute | solution.py:53
  122.3 9.8 %collective-permute-start.20 = (bf16[192,512]{1,0:T(8,128)(2,1)}, bf16[192,512]{1,0:T(8,128)(2,1)}, u32[]{:S(2)}, u32[]{:S(2)}) collective-permute-start(bf16[192,512]{1,0:T(8,128)(2,1)} %get-tuple-element.122.refs_1_), channel_id=1, source_target_pairs={{0,4},{4,0},{8,12},{12,8},{1,5},{5,1},{9,13},{13,9},{2,6},{6,2},{1... | collective-permute-start | bytes 589832 | tf_op jit(solution)/shard_map/ppermute | solution.py:53
  138.2 10.7 %collective-permute-start.24 = (bf16[48,1024]{1,0:T(8,128)(2,1)S(1)}, bf16[48,1024]{1,0:T(8,128)(2,1)S(1)}, u32[]{:S(2)}, u32[]{:S(2)}) collective-permute-start(bf16[48,1024]{1,0:T(8,128)(2,1)S(1)} %get-tuple-element.125), channel_id=1, source_target_pairs={{0,2},{1,3},{2,0},{3,1},{4,6},{5,7},{6,4},{7,5},{8,10},{9,11},{10,... | collective-permute-start | bytes 294920 | tf_op jit(solution)/shard_map/ppermute | solution.py:53
  163.8 10.8 %collective-permute-start.30 = (bf16[48,1024]{1,0:T(8,128)(2,1)S(1)}, bf16[48,1024]{1,0:T(8,128)(2,1)S(1)}, u32[]{:S(2)}, u32[]{:S(2)}) collective-permute-start(bf16[48,1024]{1,0:T(8,128)(2,1)S(1)} %get-tuple-element.131), channel_id=1, source_target_pairs={{0,2},{1,3},{2,0},{3,1},{4,6},{5,7},{6,4},{7,5},{8,10},{9,11},{10,... | collective-permute-start | bytes 294920 | tf_op jit(solution)/shard_map/ppermute | solution.py:53
  223.7 116.1 %reduce-scatter.5.cloned.1.call-start = ((), (), s32[]{:S(2)}) async-start(), calls=%async_computation.6 | async-start | bytes 2359296 | tf_op jit(solution)/shard_map/reduce_scatter | solution.py:164
  223.9 10.5 %collective-permute-start.47 = (bf16[48,1024]{1,0:T(8,128)(2,1)}, bf16[48,1024]{1,0:T(8,128)(2,1)S(1)}, u32[]{:S(2)}, u32[]{:S(2)}) collective-permute-start(bf16[48,1024]{1,0:T(8,128)(2,1)} %copy-done.62), channel_id=1, source_target_pairs={{0,2},{1,3},{2,0},{3,1},{4,6},{5,7},{6,4},{7,5},{8,10},{9,11},{10,... | collective-permute-start | bytes 294920 | tf_op jit(solution)/shard_map/ppermute | solution.py:53
  252.1 9.4 %collective-permute-start.53 = (bf16[48,1024]{1,0:T(8,128)(2,1)S(1)}, bf16[48,1024]{1,0:T(8,128)(2,1)S(1)}, u32[]{:S(2)}, u32[]{:S(2)}) collective-permute-start(bf16[48,1024]{1,0:T(8,128)(2,1)S(1)} %get-tuple-element.163), channel_id=1, source_target_pairs={{0,2},{1,3},{2,0},{3,1},{4,6},{5,7},{6,4},{7,5},{8,10},{9,11},{10,... | collective-permute-start | bytes 294920 | tf_op jit(solution)/shard_map/ppermute | solution.py:53
  286.9 95.2 %reduce-scatter.11.cloned.1.call-start = ((), (), s32[]{:S(2)}) async-start(), calls=%async_computation.9 | async-start | bytes 4718592 | tf_op jit(solution)/shard_map/reduce_scatter | solution.py:150
  290.4 146.9 %reduce-scatter.9.cloned.1.call-start = ((), (), s32[]{:S(2)}) async-start(), calls=%async_computation.8 | async-start | bytes 4718592 | tf_op jit(solution)/shard_map/reduce_scatter | solution.py:150
  296.0 16.8 %collective-permute-start.34 = (bf16[48,1024]{1,0:T(8,128)(2,1)S(1)}, bf16[48,1024]{1,0:T(8,128)(2,1)S(1)}, u32[]{:S(2)}, u32[]{:S(2)}) collective-permute-start(bf16[48,1024]{1,0:T(8,128)(2,1)S(1)} %copy-done.44), channel_id=1, source_target_pairs={{0,3},{1,2},{2,1},{3,0},{4,7},{5,6},{6,5},{7,4},{8,11},{9,10},{10,... | collective-permute-start | bytes 294920 | tf_op jit(solution)/shard_map/ppermute | solution.py:53
  297.5 15.4 %collective-permute-start.33 = (bf16[48,1024]{1,0:T(8,128)(2,1)S(1)}, bf16[48,1024]{1,0:T(8,128)(2,1)S(1)}, u32[]{:S(2)}, u32[]{:S(2)}) collective-permute-start(bf16[48,1024]{1,0:T(8,128)(2,1)S(1)} %copy-done.44), channel_id=1, source_target_pairs={{0,2},{1,3},{2,0},{3,1},{4,6},{5,7},{6,4},{7,5},{8,10},{9,11},{10,... | collective-permute-start | bytes 294920 | tf_op jit(solution)/shard_map/ppermute | solution.py:53
  297.5 15.4 %collective-permute-start.32 = (bf16[48,1024]{1,0:T(8,128)(2,1)S(1)}, bf16[48,1024]{1,0:T(8,128)(2,1)S(1)}, u32[]{:S(2)}, u32[]{:S(2)}) collective-permute-start(bf16[48,1024]{1,0:T(8,128)(2,1)S(1)} %copy-done.44), channel_id=1, source_target_pairs={{0,1},{1,0},{2,3},{3,2},{4,5},{5,4},{6,7},{7,6},{8,9},{9,8},{10,11... | collective-permute-start | bytes 294920 | tf_op jit(solution)/shard_map/ppermute | solution.py:53
  315.0 9.9 %collective-permute-start.61 = (bf16[48,1024]{1,0:T(8,128)(2,1)S(1)}, bf16[48,1024]{1,0:T(8,128)(2,1)S(1)}, u32[]{:S(2)}, u32[]{:S(2)}) collective-permute-start(bf16[48,1024]{1,0:T(8,128)(2,1)S(1)} %get-tuple-element.176), channel_id=1, source_target_pairs={{0,2},{1,3},{2,0},{3,1},{4,6},{5,7},{6,4},{7,5},{8,10},{9,11},{10,... | collective-permute-start | bytes 294920 | tf_op jit(solution)/shard_map/ppermute | solution.py:53
  315.3 9.5 %collective-permute-start.62 = (bf16[48,1024]{1,0:T(8,128)(2,1)S(1)}, bf16[48,1024]{1,0:T(8,128)(2,1)S(1)}, u32[]{:S(2)}, u32[]{:S(2)}) collective-permute-start(bf16[48,1024]{1,0:T(8,128)(2,1)S(1)} %get-tuple-element.177), channel_id=1, source_target_pairs={{0,3},{1,2},{2,1},{3,0},{4,7},{5,6},{6,5},{7,4},{8,11},{9,10},{10,... | collective-permute-start | bytes 294920 | tf_op jit(solution)/shard_map/ppermute | solution.py:53
  317.5 13.2 %collective-permute-start.67 = (f32[12,128]{1,0:T(8,128)S(1)}, f32[12,128]{1,0:T(8,128)S(1)}, u32[]{:S(2)}, u32[]{:S(2)}) collective-permute-start(f32[12,128]{1,0:T(8,128)S(1)} %slice_add_fusion), channel_id=1, source_target_pairs={{0,2},{1,3},{2,0},{3,1},{4,6},{5,7},{6,4},{7,5},{8,10},{9,11},{10,... | collective-permute-start | bytes 18440 | tf_op jit(solution)/shard_map/ppermute | solution.py:53
  326.9 9.6 %collective-permute-start.64 = (bf16[48,1024]{1,0:T(8,128)(2,1)S(1)}, bf16[48,1024]{1,0:T(8,128)(2,1)S(1)}, u32[]{:S(2)}, u32[]{:S(2)}) collective-permute-start(bf16[48,1024]{1,0:T(8,128)(2,1)S(1)} %add_convert_fusion.2), channel_id=1, source_target_pairs={{0,2},{1,3},{2,0},{3,1},{4,6},{5,7},{6,4},{7,5},{8,10},{9,11},{10,... | collective-permute-start | bytes 294920 | tf_op jit(solution)/shard_map/ppermute | solution.py:53
  (124 other events, 787.0 us)
Sparse Core Ops, SparseCore 0:
  10.5 47.2 all-gather.7
  60.2 26.0 all-gather.5
  88.7 42.1 all-gather.9
  223.8 39.9 reduce-scatter.6
  287.0 40.4 reduce-scatter.4
  330.8 51.3 reduce-scatter.10
  385.8 51.3 reduce-scatter.8

commit v2 on v1

v2 whole, which is shorter than its diff:
```python
import functools

import jax
import jax.numpy as jnp
from jax import lax
from jax.experimental import pallas as pl
from jax.experimental.pallas import tpu as pltpu
from jax.sharding import PartitionSpec as P

HD = 64
LANES = 128
SCORE_FLOOR = -1e30
PLANE = ("shard", "ctx")
BF = jnp.bfloat16
F32 = jnp.float32
VMEM_GRANT = 16 * 1024 * 1024


def dot(left, right):
    return jnp.dot(left, right, preferred_element_type=F32)


def dot_nt(left, right):
    return lax.dot_general(left, right, (((1,), (1,)), ((), ())), preferred_element_type=F32)


def dot_tn(left, right):
    return lax.dot_general(left, right, (((0,), (0,)), ((), ())), preferred_element_type=F32)


def sds(shape, kind):
    return jax.ShapeDtypeStruct(shape, kind)


def whole():
    return pl.BlockSpec(memory_space=pltpu.VMEM)


def call(body, out_shape, *operands, flops=0, scratch=(), name=None):
    moved = sum(o.size * o.dtype.itemsize for o in operands)
    moved += sum(o.size * o.dtype.itemsize for o in out_shape)
    scalar = pl.BlockSpec(memory_space=pltpu.SMEM)
    return pl.pallas_call(
        body,
        out_shape=out_shape,
        in_specs=[scalar if o.dtype == jnp.int32 and o.ndim == 1 else whole() for o in operands],
        out_specs=[whole() for _ in out_shape],
        scratch_shapes=scratch,
        compiler_params=pltpu.CompilerParams(vmem_limit_bytes=VMEM_GRANT),
        cost_estimate=pl.CostEstimate(flops=flops, bytes_accessed=moved, transcendentals=0),
        name=name,
    )(*operands)


def tie(value, after):
    return lax.optimization_barrier((value, after))[0]


def swap(value, axis, size, flip):
    return lax.ppermute(value, axis, [(i, i ^ flip) for i in range(size)])


def swap_all(pieces, axis, size):
    order = [k for k in (2, 3, 1) if k < size] + list(range(4, size))
    got = {k: swap(pieces[k], axis, size, k) for k in order}
    return [got[k] for k in range(1, size)]


def pick(blocks, index):
    return lax.dynamic_index_in_dim(blocks, index, 0, False)


def reorder(blocks, me):
    return jnp.stack([pick(blocks, me ^ k) for k in range(blocks.shape[0])])


def pack_in(matrix):
    c, rows, cols = matrix.shape
    return matrix.reshape(c, rows, cols // LANES, LANES).transpose(0, 2, 1, 3).reshape(-1, LANES)


def unpack_in(packed, c, rows, cols):
    return (
        packed.reshape(c, cols // LANES, rows, LANES).transpose(0, 2, 1, 3).reshape(c, rows, cols)
    )


def blocks_of_rows(matrix):
    c, depth, cols = matrix.shape
    cut = matrix.reshape(c, depth // LANES, LANES, cols // LANES, LANES)
    return cut.transpose(1, 0, 3, 2, 4).reshape(depth // LANES, -1, LANES)


def rows_of_blocks(packed, c, cols):
    blocks = packed.shape[0]
    cut = packed.reshape(blocks, c, cols // LANES, LANES, LANES)
    return cut.transpose(1, 0, 3, 2, 4).reshape(c, blocks * LANES, cols)


def blocks_of_cols(matrix):
    rows, width = matrix.shape
    return matrix.reshape(rows, width // LANES, LANES).transpose(1, 0, 2)


def cols_of_blocks(packed):
    blocks, rows, _ = packed.shape
    return packed.transpose(1, 0, 2).reshape(rows, blocks * LANES)


def gather_first(attn_in, attn_out, small, me, fast):
    if not fast:
        gains, shifts, ff_bias, attn_bias = small
        layers, _, share = gains.shape
        rows = jnp.concatenate(
            [
                gains.reshape(2 * layers, share),
                shifts.reshape(4 * layers, share),
                ff_bias.reshape(layers, -1),
            ],
            axis=0,
        )
        rows = lax.all_gather(rows, PLANE, axis=1, tiled=True)
        bias = lax.all_gather(attn_bias, PLANE, axis=3, tiled=True)
        return gather_attn(attn_in, attn_out, 0, fast), rows, bias.reshape(layers, 2, -1)
    layers = attn_in.shape[0]
    count = 3 * attn_in.shape[3] + attn_out.shape[1] + 32
    (own,) = call(
        pack_first_body,
        [sds((count, LANES), BF)],
        attn_in,
        attn_out,
        *small,
        scratch=[pltpu.VMEM((32, LANES), F32)],
        name="pack_first",
    )
    half = count // 2
    over_x = swap(own, "shard", 2, 1)
    over_y = swap(own, "ctx", 4, 2)
    first = swap(over_y[:half], "shard", 2, 1)
    second = swap(over_x[half:], "ctx", 4, 2)
    near = [own, over_y, over_x, first, second]
    far = [swap(piece, "ctx", 4, 1) for piece in near]
    (natural,) = call(
        assemble_body, [sds((8, count, LANES), BF)], me.reshape(1), *near, *far, name="assemble"
    )
    small_rows = natural[:, -32:].transpose(1, 0, 2)
    used = 7 * layers
    rows = small_rows[:used].reshape(used, -1)
    bias = small_rows[used : used + 2 * layers, :, : small[3].shape[3]]
    return natural, rows, bias.reshape(layers, 2, -1)


def gather_attn(attn_in, attn_out, layer, fast):
    if not fast:
        full = lax.all_gather(attn_in[layer], PLANE, axis=1, tiled=True)
        out = lax.all_gather(attn_out[layer], PLANE, axis=1, tiled=True)
        return jnp.concatenate([blocks_of_rows(full), blocks_of_cols(out)], axis=1)
    count = 3 * attn_in.shape[3] + attn_out.shape[1]
    (own,) = call(
        functools.partial(pack_attn_body, layer),
        [sds((count, LANES), BF)],
        attn_in,
        attn_out,
        name="pack_attention",
    )
    return lax.all_gather(own, PLANE, axis=0, tiled=False)


def gather_ff(ff_in, ff_out, layer, fast):
    if not fast:
        up = lax.all_gather(ff_in[layer], PLANE, axis=0, tiled=True)
        down = lax.all_gather(ff_out[layer], PLANE, axis=1, tiled=True)
        return jnp.concatenate([blocks_of_rows(up[None]), blocks_of_cols(down)], axis=1)
    (own,) = call(
        functools.partial(pack_ff_body, layer),
        [sds((2 * ff_in.shape[2], LANES), BF)],
        ff_in,
        ff_out,
        name="pack_feed_forward",
    )
    return lax.all_gather(own, PLANE, axis=0, tiled=False)


def scatter_natural(packed, fast):
    return lax.psum_scatter(packed, PLANE, scatter_dimension=0, tiled=False).astype(F32)


def scatter_permute(near, far):
    _, count, _ = near.shape
    half = count // 2
    rest = count - half
    got = swap(far, "ctx", 4, 1)
    keep_a, send_a, keep_b, send_b = call(
        reduce_core_body,
        [
            sds((2, half, LANES), F32),
            sds((2, half, LANES), BF),
            sds((2, rest, LANES), F32),
            sds((2, rest, LANES), BF),
        ],
        near,
        got,
        name="reduce_core",
    )
    got_a = swap(send_a, "shard", 2, 1)
    got_b = swap(send_b, "ctx", 4, 2)
    keep_a, send_a, keep_b, send_b = call(
        reduce_plane_body,
        [
            sds((half, LANES), F32),
            sds((half, LANES), BF),
            sds((rest, LANES), F32),
            sds((rest, LANES), BF),
        ],
        keep_a,
        got_a,
        keep_b,
        got_b,
        name="reduce_plane",
    )
    got_a = swap(send_a, "ctx", 4, 2)
    got_b = swap(send_b, "shard", 2, 1)
    (own,) = call(
        reduce_last_body,
        [sds((count, LANES), F32)],
        keep_a,
        got_a,
        keep_b,
        got_b,
        name="reduce_last",
    )
    return own


def cut_ff(own, hidden):
    return unpack_in(own[:hidden], 1, LANES, hidden)[0], own[hidden:]


def cut_attn(own, width):
    cut = 3 * width
    return unpack_in(own[:cut], 3, LANES, width), own[cut : cut + width]


def scatter_whole_ff(packed, hidden):
    up = rows_of_blocks(packed[:, :hidden], 1, hidden)[0]
    down = cols_of_blocks(packed[:, hidden:])
    return (
        lax.psum_scatter(up, PLANE, scatter_dimension=0, tiled=True).astype(F32),
        lax.psum_scatter(down, PLANE, scatter_dimension=1, tiled=True).astype(F32),
    )


def scatter_whole_attn(packed, width):
    cut = 3 * width
    stack = rows_of_blocks(packed[:, :cut], 3, width)
    out = cols_of_blocks(packed[:, cut : cut + width])
    return (
        lax.psum_scatter(stack, PLANE, scatter_dimension=1, tiled=True).astype(F32),
        lax.psum_scatter(out, PLANE, scatter_dimension=1, tiled=True).astype(F32),
    )


def join(refs, target):
    step = refs[0].shape[0]
    for k, ref in enumerate(refs):
        target[k * step : (k + 1) * step, :] = ref[...]


def split_rows(value, refs, columns=slice(None)):
    step = refs[0].shape[0]
    for k, ref in enumerate(refs):
        ref[:, columns] = value[k * step : (k + 1) * step].astype(ref.dtype)


def in_matrix(w, c, halves):
    depth = w.shape[0] * LANES
    return jnp.concatenate(
        [
            w[:, (c * halves + h) * LANES : (c * halves + h + 1) * LANES, :].reshape(depth, LANES)
            for h in range(halves)
        ],
        axis=1,
    )


def up_pair(w, pair):
    depth = w.shape[0] * LANES
    return jnp.concatenate(
        [w[:, n * LANES : (n + 1) * LANES, :].reshape(depth, LANES) for n in (2 * pair, 2 * pair + 1)],
        axis=1,
    )


def down_pair(w, pair, first, count):
    return jnp.concatenate(
        [w[s, first : first + count, :] for s in (2 * pair, 2 * pair + 1)], axis=1
    )


def pack_attn_body(layer, attn_in, attn_out, out):
    _, _, depth, width = attn_in.shape
    halves = width // LANES
    for c in range(3):
        for h in range(halves):
            first = (c * halves + h) * depth
            out[first : first + depth, :] = attn_in[layer, c, :, h * LANES : (h + 1) * LANES]
    first = 3 * halves * depth
    out[first : first + attn_out.shape[1], :] = attn_out[layer]


def pack_first_body(attn_in, attn_out, gains, shifts, ff_bias, attn_bias, out, rows):
    pack_attn_body(0, attn_in, attn_out, out)
    layers = gains.shape[0]
    rows[...] = jnp.zeros_like(rows)
    for l in range(layers):
        rows[2 * l : 2 * l + 2, :] = gains[l].astype(F32)
        first = 2 * layers + 4 * l
        rows[first : first + 4, :] = shifts[l].astype(F32)
        first = 6 * layers + l
        rows[first : first + 1, :] = ff_bias[l].astype(F32)
        for c in range(2):
            first = 7 * layers + 2 * l + c
            rows[first : first + 1, : attn_bias.shape[3]] = attn_bias[l, c].astype(F32)
    out[out.shape[0] - 32 :, :] = rows[...].astype(BF)


def pack_ff_body(layer, ff_in, ff_out, out):
    depth, hidden = ff_in.shape[1:]
    for n in range(hidden // LANES):
        out[n * depth : (n + 1) * depth, :] = ff_in[layer, :, n * LANES : (n + 1) * LANES]
    out[hidden : 2 * hidden, :] = ff_out[layer]


def assemble_body(me, *refs):
    near, far, out = refs[:5], refs[5:10], refs[10]
    half = near[3].shape[0]
    for flip, pieces in ((0, near), (1, far)):
        for j in range(3):
            out[me[0] ^ (2 * j + flip)] = pieces[j][...]
        out[me[0] ^ (6 + flip), :half, :] = pieces[3][...]
        out[me[0] ^ (6 + flip), half:, :] = pieces[4][...]


def reduce_core_body(near, got, keep_a, send_a, keep_b, send_b):
    half = keep_a.shape[1]
    for j in range(4):
        head = near[j, :half, :].astype(F32) + got[j, :half, :].astype(F32)
        tail = near[j, half:, :].astype(F32) + got[j, half:, :].astype(F32)
        if j < 2:
            keep_a[j] = head
        else:
            send_a[j - 2] = head.astype(BF)
        if j % 2 == 0:
            keep_b[j // 2] = tail
        else:
            send_b[j // 2] = tail.astype(BF)


def reduce_plane_body(near_a, got_a, near_b, got_b, keep_a, send_a, keep_b, send_b):
    for near, got, keep, send in (
        (near_a, got_a, keep_a, send_a),
        (near_b, got_b, keep_b, send_b),
    ):
        keep[...] = near[0] + got[0].astype(F32)
        send[...] = (near[1] + got[1].astype(F32)).astype(BF)


def reduce_last_body(keep_a, got_a, keep_b, got_b, out):
    half = keep_a.shape[0]
    out[:half, :] = keep_a[...] + got_a[...].astype(F32)
    out[half:, :] = keep_b[...] + got_b[...].astype(F32)


def put(outs, me, pair, rows, even, odd):
    if me is None:
        outs[0][2 * pair, rows, :] = even
        outs[0][2 * pair + 1, rows, :] = odd
        return
    near, far = outs
    slot = pair ^ (me[0] // 2)
    turned = me[0] % 2 == 1
    near[slot, rows, :] = jnp.where(turned, odd, even)
    far[slot, rows, :] = jnp.where(turned, even, odd)


def qkv_body(n, *refs):
    x_refs, (w, bias, x_out, q_out, kv_out) = refs[:n], refs[n:]
    join(x_refs, x_out)
    x = x_out[...]
    width = q_out.shape[1]
    halves = width // LANES
    q_out[...] = (dot(x, in_matrix(w, 0, halves)) + bias[0:1, :]).astype(BF)
    kv_out[:, :width] = dot(x, in_matrix(w, 1, halves)).astype(BF)
    kv_out[:, width:] = (dot(x, in_matrix(w, 2, halves)) + bias[1:2, :]).astype(BF)


def attend_body(m, n, *refs):
    q_ref, kv_refs = refs[0], refs[1 : 1 + m]
    seg_q, seg_k, w = refs[1 + m : 4 + m]
    o_out, lse_out, kv_all = refs[4 + m : 7 + m]
    pieces = refs[7 + m :]
    join(kv_refs, kv_all)
    width = q_ref.shape[1]
    same = seg_q[...] == seg_k[...]
    for h in range(width // HD):
        cols = slice(h * HD, (h + 1) * HD)
        vcols = slice(width + h * HD, width + (h + 1) * HD)
        s = dot_nt(q_ref[:, cols], kv_all[:, cols]) * HD ** (-0.5)
        s = jnp.where(same, s, SCORE_FLOOR)
        top = jnp.max(s, axis=-1, keepdims=True)
        e = jnp.exp(s - top)
        total = jnp.sum(e, axis=-1, keepdims=True)
        prob = (e / total).astype(BF)
        lse_out[:, h : h + 1] = top + jnp.log(total)
        o_out[:, cols] = dot(prob, kv_all[:, vcols]).astype(BF)
    o = o_out[...]
    for pair in range(w.shape[0] // 2):
        span = slice(2 * pair * LANES, (2 * pair + 2) * LANES)
        split_rows(dot(o, down_pair(w, pair, 3 * width, width)), pieces, span)


def norm_body(n, *refs):
    base, own = refs[0], refs[1]
    others = refs[2 : 1 + n]
    shift, gain, centre_shift, out, out_low, normed, inverse = refs[1 + n :]
    r = base[...] + own[...]
    for other in others:
        r = r + other[...].astype(F32)
    r = r + shift[...]
    centre = r - jnp.mean(r, axis=-1, keepdims=True)
    inv = lax.rsqrt(jnp.mean(centre * centre, axis=-1, keepdims=True) + 1e-12)
    norm = centre * inv
    y = norm * gain[...] + centre_shift[...]
    out[...] = y
    out_low[...] = y.astype(BF)
    normed[...] = norm
    inverse[...] = jnp.broadcast_to(inv, inverse.shape)


def ff_body(n, *refs):
    h_refs = refs[:n]
    w, bias, h_out, slope_out, act_out = refs[n : n + 5]
    pieces = refs[n + 5 :]
    join(h_refs, h_out)
    h = h_out[...]
    hidden = act_out.shape[1]
    for pair in range(hidden // (2 * LANES)):
        span = slice(2 * pair * LANES, (2 * pair + 2) * LANES)
        u = dot(h, up_pair(w, pair)) + bias[:, span]
        cdf = 0.5 * (1.0 + lax.erf(u * (0.5**0.5)))
        act_out[:, span] = (u * cdf).astype(BF)
        slope_out[:, span] = cdf + u * (jnp.exp(-0.5 * u * u) * 0.3989422804014327)
    act = act_out[...]
    for pair in range(w.shape[0] // 2):
        span = slice(2 * pair * LANES, (2 * pair + 2) * LANES)
        split_rows(dot(act, down_pair(w, pair, hidden, hidden)), pieces, span)


def norm_back_body(n, *refs):
    base, own = refs[0], refs[1 : 2 if n else 1]
    others = refs[2 : 1 + n] if n else ()
    normed, inverse, gain, grad, grad_low, sums = refs[1 + n :]
    dy = base[...]
    for ref in own:
        dy = dy + ref[...]
    for ref in others:
        dy = dy + ref[...].astype(F32)
    norm = normed[...]
    e = dy * gain[...]
    dr = inverse[:, 0:1] * (
        e
        - jnp.mean(e, axis=-1, keepdims=True)
        - norm * jnp.mean(e * norm, axis=-1, keepdims=True)
    )
    grad[...] = dr
    grad_low[...] = dr.astype(BF)
    sums[...] = jnp.zeros_like(sums)
    sums[0:1, :] = jnp.sum(dy * norm, axis=0, keepdims=True)
    sums[1:2, :] = jnp.sum(dy, axis=0, keepdims=True)
    sums[2:3, :] = jnp.sum(dr, axis=0, keepdims=True)


def ff_back_body(n, *refs):
    g_refs = refs[:n]
    w, slope, g_out, du_out, bias_out = refs[n : n + 5]
    pieces = refs[n + 5 : 2 * n + 5]
    total = refs[2 * n + 5]
    join(g_refs, g_out)
    hidden = du_out.shape[1]
    for pair in range(w.shape[0] // 2):
        span = slice(2 * pair * LANES, (2 * pair + 2) * LANES)
        term = dot_nt(g_out[:, span], down_pair(w, pair, hidden, hidden))
        total[...] = term if pair == 0 else total[...] + term
    du = (total[...] * slope[...]).astype(BF)
    du_out[...] = du
    bias_out[...] = jnp.broadcast_to(
        jnp.sum(du.astype(F32), axis=0, keepdims=True), bias_out.shape
    )
    for pair in range(hidden // (2 * LANES)):
        span = slice(2 * pair * LANES, (2 * pair + 2) * LANES)
        term = dot_nt(du_out[:, span], up_pair(w, pair))
        total[...] = term if pair == 0 else total[...] + term
    split_rows(total[...], pieces)


def ff_grad_body(turn, *refs):
    me = refs[0] if turn else None
    h_ref, act_ref, g_ref, du_ref = refs[turn : turn + 4]
    outs = refs[turn + 4 :]
    h, act = h_ref[...], act_ref[...]
    hidden = act.shape[1]
    blocks = g_ref.shape[1] // LANES
    for pair in range(hidden // (2 * LANES)):
        span = slice(2 * pair * LANES, (2 * pair + 2) * LANES)
        grad = dot_tn(h, du_ref[:, span]).astype(BF)
        for j in range(2):
            rows = slice((2 * pair + j) * LANES, (2 * pair + j + 1) * LANES)
            cols = slice(j * LANES, (j + 1) * LANES)
            for q in range(blocks // 2):
                first = 2 * q * LANES
                put(
                    outs,
                    me,
                    q,
                    rows,
                    grad[first : first + LANES, cols],
                    grad[first + LANES : first + 2 * LANES, cols],
                )
    for pair in range(blocks // 2):
        span = slice(2 * pair * LANES, (2 * pair + 2) * LANES)
        grad = dot_tn(act, g_ref[:, span]).astype(BF)
        put(outs, me, pair, slice(hidden, 2 * hidden), grad[:, :LANES], grad[:, LANES:])


def attend_back_body(n, m, *refs):
    g_refs = refs[:n]
    w, q_ref, kv, lse, seg_q, seg_k, g_out, dq_out, near_out, far_out, do_ref, grads = refs[n:]
    join(g_refs, g_out)
    width = q_ref.shape[1]
    scale = HD ** (-0.5)
    for pair in range(w.shape[0] // 2):
        span = slice(2 * pair * LANES, (2 * pair + 2) * LANES)
        term = dot_nt(g_out[:, span], down_pair(w, pair, 3 * width, width))
        total = term if pair == 0 else total + term
    do_ref[...] = total.astype(BF)
    same = seg_q[...] == seg_k[...]
    for h in range(width // HD):
        cols = slice(h * HD, (h + 1) * HD)
        vcols = slice(width + h * HD, width + (h + 1) * HD)
        s = dot_nt(q_ref[:, cols], kv[:, cols]) * scale
        s = jnp.where(same, s, SCORE_FLOOR)
        prob = jnp.exp(s - lse[:, h : h + 1])
        dp = dot_nt(do_ref[:, cols], kv[:, vcols])
        row = jnp.sum(dp * prob, axis=-1, keepdims=True)
        ds = (prob * (dp - row)).astype(BF)
        dq_out[:, cols] = (dot(ds, kv[:, cols]) * scale).astype(BF)
        grads[:, cols] = dot_tn(ds, q_ref[:, cols]) * scale
        grads[:, vcols] = dot_tn(prob.astype(BF), do_ref[:, cols])
    step = q_ref.shape[0]
    for j in range(m // 2):
        near_out[j] = grads[2 * j * step : (2 * j + 1) * step, :]
        far_out[j] = grads[(2 * j + 1) * step : (2 * j + 2) * step, :].astype(BF)


def qkv_back_body(n, near, got, last, dq, w, kv_out, *pieces):
    width = dq.shape[1]
    halves = width // LANES
    kv_out[...] = (near[0] + got[0].astype(F32) + last[...].astype(F32)).astype(BF)
    total = dot_nt(dq[...], in_matrix(w, 0, halves))
    total = total + dot_nt(kv_out[:, :width], in_matrix(w, 1, halves))
    total = total + dot_nt(kv_out[:, width:], in_matrix(w, 2, halves))
    split_rows(total, pieces)


def attn_grad_body(turn, *refs):
    me = refs[0] if turn else None
    x_ref, dq, dkv, o_ref, g_ref = refs[turn : turn + 5]
    lines, biases = refs[turn + 5 : turn + 7] if turn else (None, None)
    outs, sums = refs[5 + 3 * turn : -1], refs[-1]
    x = x_ref[...]
    width = dq.shape[1]
    halves = width // LANES
    blocks = g_ref.shape[1] // LANES
    for c in range(3):
        d = dq[...] if c == 0 else dkv[:, (c - 1) * width : c * width]
        grad = dot_tn(x, d).astype(BF)
        for h in range(halves):
            rows = slice((c * halves + h) * LANES, (c * halves + h + 1) * LANES)
            cols = slice(h * LANES, (h + 1) * LANES)
            for q in range(blocks // 2):
                first = 2 * q * LANES
                put(
                    outs,
                    me,
                    q,
                    rows,
                    grad[first : first + LANES, cols],
                    grad[first + LANES : first + 2 * LANES, cols],
                )
    o = o_ref[...]
    for pair in range(blocks // 2):
        span = slice(2 * pair * LANES, (2 * pair + 2) * LANES)
        grad = dot_tn(o, g_ref[:, span]).astype(BF)
        put(outs, me, pair, slice(3 * width, 4 * width), grad[:, :LANES], grad[:, LANES:])
    sums[...] = jnp.zeros_like(sums)
    sums[0:1, :] = jnp.sum(dq[...].astype(F32), axis=0, keepdims=True)
    sums[1:2, :] = jnp.sum(dkv[:, width:].astype(F32), axis=0, keepdims=True)
    if turn:
        count = lines.shape[0]
        both = jnp.concatenate([sums[...], biases[...]], axis=0).astype(BF)
        low = lines[...].astype(BF)
        per = blocks // halves
        for pair in range(blocks // 2):
            cut = [
                jnp.concatenate(
                    [
                        low[:, s * LANES : (s + 1) * LANES],
                        both[:, s // per * LANES : (s // per + 1) * LANES],
                    ],
                    axis=0,
                )
                for s in (2 * pair, 2 * pair + 1)
            ]
            put(outs, me, pair, slice(4 * width, 4 * width + count + 16), *cut)


def shards(sizes, *args):
    shard_n, ctx_n, tp_n = sizes
    (
        hidden_in,
        seg_ids,
        attn_in,
        attn_bias,
        attn_out,
        ff_in,
        ff_bias,
        ff_out,
        gains,
        shifts,
        cotangent,
    ) = args
    packs, tok, depth = hidden_in.shape
    layers = attn_in.shape[0]
    width = attn_in.shape[3]
    hidden = ff_in.shape[2]
    plane_n = shard_n * ctx_n
    blocks = depth // LANES
    fast = (shard_n, ctx_n, blocks, layers) == (2, 4, 8, 2)
    step = tok // tp_n
    share = depth // plane_n
    keys = ctx_n * tok
    heads = width // HD
    tp_me = lax.axis_index("tp")
    ctx_me = lax.axis_index("ctx")
    me = (lax.axis_index("shard") * ctx_n + ctx_me).astype(jnp.int32)

    first, rows, qv_bias = gather_first(
        attn_in, attn_out, (gains, shifts, ff_bias, attn_bias), me, fast
    )
    ff_w = [None] * layers
    attn_w = [first] + [None] * (layers - 1)
    for l in range(layers):
        if l > 0:
            attn_w[l] = gather_attn(attn_in, attn_out, l, fast)
        ff_w[l] = gather_ff(ff_in, ff_out, l, fast)

    rows_f = rows.astype(F32)
    qv_bias = qv_bias.astype(F32)
    gain_row = lambda l, j: rows_f[2 * l + j][None]
    shift_row = lambda l, j: rows_f[2 * layers + 4 * l + j][None]
    up_bias = lambda l: rows_f[6 * layers + l][None]

    x_pieces = reorder(hidden_in.reshape(tp_n, step, depth), tp_me)
    seg_cut = reorder(seg_ids.reshape(ctx_n, tp_n, step), ctx_me)
    seg_cut = reorder(seg_cut.transpose(1, 0, 2), tp_me).transpose(1, 0, 2)
    seg_k = seg_cut.reshape(1, -1)
    seg_q = seg_cut[0].reshape(tok, 1)

    def piece_shapes():
        return [sds((step, depth), F32)] + [sds((step, depth), BF)] * (tp_n - 1)

    def matmul(*dims):
        return 2 * functools.reduce(lambda a, b: a * b, dims)

    def spread(piece):
        return [piece] + swap_all([piece] * tp_n, "tp", tp_n)

    def norm(base, own, got, shift, gain, move):
        return call(
            functools.partial(norm_body, tp_n),
            [
                sds((step, depth), F32),
                sds((step, depth), BF),
                sds((step, depth), F32),
                sds((step, LANES), F32),
            ],
            base,
            own,
            *got,
            shift,
            gain,
            move,
            name="norm",
        )

    def norm_back(base, pieces, normed, inverse, gain):
        return call(
            functools.partial(norm_back_body, len(pieces)),
            [sds((step, depth), F32), sds((step, depth), BF), sds((8, depth), F32)],
            base,
            *pieces,
            normed,
            inverse,
            gain,
            name="norm_back",
        )

    base = x_pieces[0].astype(F32)
    low = [x_pieces[k] for k in range(tp_n)]
    kept = []
    for l in range(layers):
        x, q, kv = call(
            functools.partial(qkv_body, tp_n),
            [sds((tok, depth), BF), sds((tok, width), BF), sds((tok, 2 * width), BF)],
            *low,
            attn_w[l],
            qv_bias[l],
            flops=matmul(tok, depth, 3 * width),
            name="project_in",
        )
        over_y = swap(kv, "ctx", ctx_n, 2)
        over_core = swap(kv, "ctx", ctx_n, 1)
        over_both = swap(over_y, "ctx", ctx_n, 1)
        o, lse, kv_all, *a_pieces = call(
            functools.partial(attend_body, ctx_n, tp_n),
            [sds((tok, width), BF), sds((tok, heads), F32), sds((keys, 2 * width), BF)]
            + piece_shapes(),
            q,
            kv,
            over_core,
            over_y,
            over_both,
            seg_q,
            seg_k,
            attn_w[l],
            flops=matmul(tok, keys, 2 * width) + matmul(tok, width, depth),
            name="attend",
        )
        got = swap_all(a_pieces, "tp", tp_n)
        hid, hid_low, n1, inv1 = norm(
            base, a_pieces[0], got, shift_row(l, 0), gain_row(l, 0), shift_row(l, 1)
        )
        h, slope, act, *f_pieces = call(
            functools.partial(ff_body, tp_n),
            [sds((tok, depth), BF), sds((tok, hidden), F32), sds((tok, hidden), BF)]
            + piece_shapes(),
            *spread(hid_low),
            ff_w[l],
            up_bias(l),
            flops=2 * matmul(tok, depth, hidden),
            name="feed_forward",
        )
        got = swap_all(f_pieces, "tp", tp_n)
        base, y_low, n2, inv2 = norm(
            hid, f_pieces[0], got, shift_row(l, 2), gain_row(l, 1), shift_row(l, 3)
        )
        if l < layers - 1:
            low = spread(y_low)
        kept.append((x, q, kv_all, lse, o, n1, inv1, h, slope, act, n2, inv2))

    grad = pick(cotangent.reshape(tp_n, step, depth), tp_me).astype(F32)
    terms = []
    row_sums = [None] * layers
    qv_sums = [None] * layers
    ff_grads = [None] * layers
    attn_grads = [None] * layers
    lines = []
    for l in reversed(range(layers)):
        turn = int(fast and l == 0)
        where = [me.reshape(1)] * turn
        x, q, kv_all, lse, o, n1, inv1, h, slope, act, n2, inv2 = kept[l]
        dr2, df_low, sums2 = norm_back(grad, terms, n2, inv2, gain_row(l, 1))
        df, du, sums_up, *h_pieces = call(
            functools.partial(ff_back_body, tp_n),
            [sds((tok, depth), BF), sds((tok, hidden), BF), sds((8, hidden), F32)]
            + piece_shapes(),
            *spread(df_low),
            ff_w[l],
            slope,
            flops=2 * matmul(tok, depth, hidden),
            scratch=[pltpu.VMEM((tok, hidden), F32)],
            name="feed_forward_back",
        )
        got = swap_all(h_pieces, "tp", tp_n)
        packed = call(
            functools.partial(ff_grad_body, turn),
            [sds((blocks // (1 + turn), 2 * hidden, LANES), BF)] * (1 + turn),
            *where,
            h,
            act,
            df,
            du,
            flops=2 * matmul(tok, depth, hidden),
            name="feed_forward_grad",
        )
        got = tie(got, packed)
        if turn:
            ff_grads[l] = cut_ff(scatter_permute(*packed), hidden)
        elif fast:
            ff_grads[l] = cut_ff(scatter_natural(packed[0], fast), hidden)
        else:
            ff_grads[l] = scatter_whole_ff(packed[0], hidden)
        dr1, da_low, sums1 = norm_back(dr2, [h_pieces[0], *got], n1, inv1, gain_row(l, 0))
        row_sums[l] = (sums1, sums2, sums_up)
        da, dq, near, far = call(
            functools.partial(attend_back_body, tp_n, ctx_n),
            [
                sds((tok, depth), BF),
                sds((tok, width), BF),
                sds((ctx_n // 2, tok, 2 * width), F32),
                sds((ctx_n // 2, tok, 2 * width), BF),
            ],
            *spread(da_low),
            attn_w[l],
            q,
            kv_all,
            lse,
            seg_q,
            seg_k,
            flops=5 * matmul(tok, keys, width) + matmul(tok, width, depth),
            scratch=[pltpu.VMEM((tok, width), BF), pltpu.VMEM((keys, 2 * width), F32)],
            name="attend_back",
        )
        got = swap(far, "ctx", ctx_n, 1)
        if l == layers - 1:
            low = spread(tie(y_low, far))
        if l == 0:
            norms = [s for sums1, sums2, _ in row_sums for s in (sums1[0:1], sums2[0:1])]
            for sums1, sums2, _ in row_sums:
                norms += [sums1[2:3], sums1[1:2], sums2[2:3], sums2[1:2]]
            norms = jnp.concatenate(norms, axis=0)
            flip = 1
            while flip < tp_n:
                norms = norms + swap(norms, "tp", tp_n, flip)
                flip *= 2
            lines = jnp.concatenate([norms] + [s[0:1] for _, _, s in row_sums], axis=0)
            lines = jnp.pad(lines, ((0, -lines.shape[0] % 16), (0, 0)))
        passed = (near[1] + got[1].astype(F32)).astype(BF)
        last = swap(passed, "ctx", ctx_n, 2)
        dkv, *x_pieces = call(
            functools.partial(qkv_back_body, tp_n),
            [sds((tok, 2 * width), BF)] + piece_shapes(),
            near,
            got,
            last,
            dq,
            attn_w[l],
            flops=matmul(tok, depth, 3 * width),
            name="project_in_back",
        )
        got = swap_all(x_pieces, "tp", tp_n)
        count = 4 * width + turn * (lines.shape[0] + 16 if turn else 0)
        *packed, qv_sums[l] = call(
            functools.partial(attn_grad_body, turn),
            [sds((blocks // (1 + turn), count, LANES), BF)] * (1 + turn) + [sds((8, width), F32)],
            *where,
            x,
            dq,
            dkv,
            o,
            da,
            *([lines, qv_sums[1]] if turn else []),
            flops=matmul(tok, depth, 4 * width),
            name="attend_grad",
        )
        got = tie(got, packed)
        if turn:
            own = scatter_permute(*packed)
            attn_grads[l] = cut_attn(own, width)
        elif fast:
            attn_grads[l] = cut_attn(scatter_natural(packed[0], fast), width)
        else:
            attn_grads[l] = scatter_whole_attn(packed[0], width)
        grad = dr1
        terms = [x_pieces[0], *got]

    hidden_out = reorder(jnp.stack(low), tp_me).reshape(packs, tok, depth)
    total = grad + terms[0]
    for term in terms[1:]:
        total = total + term.astype(F32)
    pieces = spread(total.astype(BF))
    grad_in = reorder(jnp.stack(pieces), tp_me).astype(F32).reshape(packs, tok, depth)

    count = lines.shape[0]
    if fast:
        lines = own[4 * width : 4 * width + count]
        narrow = width // plane_n
        bias = own[4 * width + count :].reshape(layers, 8, LANES)[:, :2]
        first = lax.rem(me, LANES // narrow) * narrow
        bias = lax.dynamic_slice_in_dim(bias, first, narrow, 2)
    else:
        lines = lax.psum_scatter(lines, PLANE, scatter_dimension=1, tiled=True)
        bias = jnp.stack([s[0:2] for s in qv_sums])
        bias = lax.psum_scatter(bias, PLANE, scatter_dimension=2, tiled=True)

    return (
        hidden_out,
        grad_in,
        jnp.stack([g[0] for g in attn_grads]),
        bias.reshape(attn_bias.shape),
        jnp.stack([g[1] for g in attn_grads]),
        jnp.stack([g[0] for g in ff_grads]),
        lines[6 * layers : 7 * layers].reshape(ff_bias.shape),
        jnp.stack([g[1] for g in ff_grads]),
        lines[: 2 * layers].reshape(gains.shape),
        lines[2 * layers : 6 * layers].reshape(shifts.shape),
    )


def solution(mesh):
    in_specs = (
        P("shard", "ctx", None),
        P("shard", None),
        P(None, None, ("shard", "ctx"), "tp"),
        P(None, None, "tp", ("shard", "ctx")),
        P(None, "tp", ("shard", "ctx")),
        P(None, ("shard", "ctx"), "tp"),
        P(None, "tp", ("shard", "ctx")),
        P(None, "tp", ("shard", "ctx")),
        P(None, None, ("shard", "ctx")),
        P(None, None, ("shard", "ctx")),
        P("shard", "ctx", None),
    )
    out_specs = (
        P("shard", "ctx", None),
        P("shard", "ctx", None),
        P(None, None, ("shard", "ctx"), "tp"),
        P(None, None, "tp", ("shard", "ctx")),
        P(None, "tp", ("shard", "ctx")),
        P(None, ("shard", "ctx"), "tp"),
        P(None, "tp", ("shard", "ctx")),
        P(None, "tp", ("shard", "ctx")),
        P(None, None, ("shard", "ctx")),
        P(None, None, ("shard", "ctx")),
    )
    sizes = (mesh.shape["shard"], mesh.shape["ctx"], mesh.shape["tp"])
    return jax.shard_map(
        functools.partial(shards, sizes),
        mesh=mesh,
        in_specs=in_specs,
        out_specs=out_specs,
        check_vma=False,
    )
```

time: 449 us -> 369 us (0.82)
  waiting for transfers between devices: 236 us -> 137 us
  starting transfers between devices: 88.2 us -> 105 us
  Pallas kernels: 30.7 us -> 39.3 us
  blocking collectives: 7.7 us -> 0 us
    reduce_scatter x4 -> x2, waiting for transfers between devices: 92.4 us -> 0.02 us  [scatter_natural(): lax.psum_scatter(packed, PLANE, scatter_dimension=0, tiled=False)]
    unnamed x153 -> x212, local copies, waits for them, and re-layouts: 32.2 us -> 50.8 us
    ppermute x68 -> x82, starting transfers between devices: 87.9 us -> 105 us  [swap(): return lax.ppermute(value, axis, [(i, i ^ flip) for i in range(size)])]
    slice x27 -> x16, local copies, waits for them, and re-layouts: 18.3 us -> 7.21 us  [the longest x4 1.78 us: shards(): norms += [sums1[2:3], sums1[1:2], sums2[2:3], sums2[1:2]]]
    all_gather x3, waiting for transfers between devices: 10.7 us -> 0.01 us  [the longest x2 0.01 us: gather_ff(): return lax.all_gather(own, PLANE, axis=0, tiled=False)]
    pallas_call x24 -> x35, Pallas kernels: 30.7 us -> 39.3 us  [call(): pl.pallas_call(body, out_shape=out_shape, in_specs=[scalar if o.dtype ==...]
    all_to_all x1 -> x0, blocking collectives: 7.7 us -> none  [shards(): lines = lax.all_to_all(lines, PLANE, 0, 0, tiled=True)]
    ppermute x68 -> x82, waiting for transfers between devices: 133 us -> 137 us  [swap(): return lax.ppermute(value, axis, [(i, i ^ flip) for i in range(size)])]
  transfers between devices with their start and end apart: 75 -> 87, of which waited for: 45 -> 43; matrix products, arithmetic and copies ran while one was open for 7% -> 5% of each run, Pallas kernels for 4% -> 7%
where the time goes in v2:
time: 369 us; the launch traced here: 367 us
  waiting for transfers between devices  137 us (37%)
  starting transfers between devices  105 us (28%)
  local copies, waits for them, and re-layouts  62.1 us (17%)
  Pallas kernels  39.3 us (11%)
  between operations  14.9 us (4%)
  other arithmetic  8.67 us (2%)
    ppermute x82, waiting for transfers between devices, swap(): return lax.ppermute(value, axis, [(i, i ^ flip) for i in range(size)])  137 us
    ppermute x82, starting transfers between devices, swap(): return lax.ppermute(value, axis, [(i, i ^ flip) for i in range(size)])  105 us
    unnamed x212, local copies, waits for them, and re-layouts  50.8 us
    pallas_call x35, Pallas kernels, call(): pl.pallas_call(body, out_shape=out_shape, in_specs=[scalar if o.dtype ==...  39.3 us
  transfers between devices with their start and end apart: 87, of which 43 were waited for; matrix products, arithmetic and copies ran while one was open for 5% of the time, Pallas kernels for 7%

profile of v2, /device:TPU:0, one launch (start us, length us, event | category | flops | bytes accessed | tf_op | source)
XLA Modules:
  0.0 367.2 jit_solution(9829845837645666212)
XLA Ops:
  12.4 3.0 collective-permute-start.1
  16.9 5.0 %collective-permute-done.1.refs_2_ = bf16[1056,128]{1,0:T(8,128)(2,1)S(1)} collective-permute-done((bf16[1056,128]{1,0:T(8,128)(2,1)S(1)}, bf16[1056,128]{1,0:T(8,128)(2,1)S(1)}, u32[]{:S(2)}, u32[]{:S(2)}) %collective-permute-start.1) | collective-permute-done | bytes 270368 | tf_op jit(solution)/shard_map/ppermute | solution.py:60
  26.1 4.6 %collective-permute-done.3.refs_4_ = bf16[528,128]{1,0:T(8,128)(2,1)S(1)} collective-permute-done((bf16[528,128]{1,0:T(8,128)(2,1)S(1)}, bf16[528,128]{1,0:T(8,128)(2,1)S(1)}, u32[]{:S(2)}, u32[]{:S(2)}) %collective-permute-start.3) | collective-permute-done | bytes 135200 | tf_op jit(solution)/shard_map/ppermute | solution.py:60
  47.1 8.2 %collective-permute-done.10.refs_3_ = bf16[192,512]{1,0:T(8,128)(2,1)S(1)} collective-permute-done((bf16[192,512]{1,0:T(8,128)(2,1)S(1)}, bf16[192,512]{1,0:T(8,128)(2,1)S(1)}, u32[]{:S(2)}, u32[]{:S(2)}) %collective-permute-start.10) | collective-permute-done | bytes 196640 | tf_op jit(solution)/shard_map/ppermute | solution.py:60
  65.7 7.1 %collective-permute-done.13.refs_3_ = bf16[48,1024]{1,0:T(8,128)(2,1)S(1)} collective-permute-done((bf16[48,1024]{1,0:T(8,128)(2,1)S(1)}, bf16[48,1024]{1,0:T(8,128)(2,1)S(1)}, u32[]{:S(2)}, u32[]{:S(2)}) %collective-permute-start.13) | collective-permute-done | bytes 98336 | tf_op jit(solution)/shard_map/ppermute | solution.py:60
  78.1 3.0 collective-permute-done.17.refs_3_
  81.2 3.5 collective-permute-done.16.refs_2_
  89.7 2.9 collective-permute-start.19
  94.8 5.1 %collective-permute-done.19.refs_3_ = bf16[48,1024]{1,0:T(8,128)(2,1)S(1)} collective-permute-done((bf16[48,1024]{1,0:T(8,128)(2,1)S(1)}, bf16[48,1024]{1,0:T(8,128)(2,1)S(1)}, u32[]{:S(2)}, u32[]{:S(2)}) %collective-permute-start.19) | collective-permute-done | bytes 98336 | tf_op jit(solution)/shard_map/ppermute | solution.py:60
  106.7 3.0 collective-permute-done.23.refs_3_
  109.7 3.0 collective-permute-done.22.refs_2_
  116.1 10.6 %collective-permute-done.25.refs_3_ = bf16[192,512]{1,0:T(8,128)(2,1)S(1)} collective-permute-done((bf16[192,512]{1,0:T(8,128)(2,1)S(1)}, bf16[192,512]{1,0:T(8,128)(2,1)S(1)}, u32[]{:S(2)}, u32[]{:S(2)}) %collective-permute-start.25) | collective-permute-done | bytes 196640 | tf_op jit(solution)/shard_map/ppermute | solution.py:60
  136.6 4.9 %collective-permute-done.28.refs_3_ = bf16[48,1024]{1,0:T(8,128)(2,1)S(1)} collective-permute-done((bf16[48,1024]{1,0:T(8,128)(2,1)S(1)}, bf16[48,1024]{1,0:T(8,128)(2,1)S(1)}, u32[]{:S(2)}, u32[]{:S(2)}) %collective-permute-start.28) | collective-permute-done | bytes 98336 | tf_op jit(solution)/shard_map/ppermute | solution.py:60
  148.8 3.4 collective-permute-done.32.refs_3_
  152.2 3.8 %collective-permute-done.31.refs_2_ = bf16[48,1024]{1,0:T(8,128)(2,1)} collective-permute-done((bf16[48,1024]{1,0:T(8,128)(2,1)}, bf16[48,1024]{1,0:T(8,128)(2,1)}, u32[]{:S(2)}, u32[]{:S(2)}) %collective-permute-start.31) | collective-permute-done | bytes 98336 | tf_op jit(solution)/shard_map/ppermute | solution.py:60
  166.7 5.0 %collective-permute-done.34.refs_3_ = bf16[48,1024]{1,0:T(8,128)(2,1)S(1)} collective-permute-done((bf16[48,1024]{1,0:T(8,128)(2,1)S(1)}, bf16[48,1024]{1,0:T(8,128)(2,1)S(1)}, u32[]{:S(2)}, u32[]{:S(2)}) %collective-permute-start.34) | collective-permute-done | bytes 98336 | tf_op jit(solution)/shard_map/ppermute | solution.py:60
  213.2 3.6 attend_back.2
  219.7 6.0 %collective-permute-done.49.last = bf16[192,512]{1,0:T(8,128)(2,1)S(1)} collective-permute-done((bf16[192,512]{1,0:T(8,128)(2,1)S(1)}, bf16[192,512]{1,0:T(8,128)(2,1)S(1)}, u32[]{:S(2)}, u32[]{:S(2)}) %collective-permute-start.49) | collective-permute-done | bytes 196640 | tf_op jit(solution)/shard_map/ppermute | solution.py:60
  235.2 5.2 %collective-permute-done.51.refs_3_ = bf16[48,1024]{1,0:T(8,128)(2,1)S(1)} collective-permute-done((bf16[48,1024]{1,0:T(8,128)(2,1)}, bf16[48,1024]{1,0:T(8,128)(2,1)S(1)}, u32[]{:S(2)}, u32[]{:S(2)}) %collective-permute-start.51) | collective-permute-done | bytes 98336 | tf_op jit(solution)/shard_map/ppermute | solution.py:60
  262.7 3.0 feed_forward_grad.3
  276.7 4.4 %attend_back.3 = (bf16[192,1024]{1,0:T(8,128)(2,1)S(1)}, bf16[192,256]{1,0:T(8,128)(2,1)S(1)}, f32[2,192,512]{2,1,0:T(8,128)S(1)}, bf16[2,192,512]{2,1,0:T(8,128)(2,1)}) custom-call(bf16[48,1024]{1,0:T(8,128)(2,1)S(1)} %get-tuple-element.224.refs_0_, bf16[48,1024]{1,0:T(8,128)(2,1)S(1)} %collective-permute-done.59.refs_1_, ...), custom_call_target="tpu_custom_call" | custom-call | flops 478150656 | bytes 5118720 | tf_op jit(solution)/shard_map/attend_back/pallas_call | solution.py:43
  289.9 3.0 collective-permute-done.68
  307.8 7.0 %collective-permute-start.45 = (bf16[48,1024]{1,0:T(8,128)(2,1)S(1)}, bf16[48,1024]{1,0:T(8,128)(2,1)S(1)}, u32[]{:S(2)}, u32[]{:S(2)}) collective-permute-start(bf16[48,1024]{1,0:T(8,128)(2,1)S(1)} %copy-done.56), channel_id=1, source_target_pairs={{0,1},{1,0},{2,3},{3,2},{4,5},{5,4},{6,7},{7,6},{8,9},{9,8},{10,11... | collective-permute-start | bytes 294920 | tf_op jit(solution)/shard_map/ppermute | solution.py:60
  334.7 11.0 %collective-permute-done.75.got_a = bf16[528,128]{1,0:T(8,128)(2,1)S(1)} collective-permute-done((bf16[528,128]{1,0:T(8,128)(2,1)S(1)}, bf16[528,128]{1,0:T(8,128)(2,1)S(1)}, u32[]{:S(2)}, u32[]{:S(2)}) %collective-permute-start.75) | collective-permute-done | bytes 135200 | tf_op jit(solution)/shard_map/ppermute | solution.py:60
  (465 shorter events, 232.8 us)
Async XLA Ops:
  7.2 77.4 %all-gather.7.cloned.1.call-start = ((), (), s32[]{:S(2)}) async-start(), calls=%async_computation.4 | async-start | bytes 4718592 | tf_op jit(solution)/shard_map/all_gather | solution.py:181
  10.2 96.4 %all-gather.9.cloned.1.call-start = ((), (), s32[]{:S(2)}) async-start(), calls=%async_computation.5 | async-start | bytes 2359296 | tf_op jit(solution)/shard_map/all_gather | solution.py:166
  11.3 137.5 %all-gather.11.cloned.1.call-start = ((), (), s32[]{:S(2)}) async-start(), calls=%async_computation.6 | async-start | bytes 4718592 | tf_op jit(solution)/shard_map/all_gather | solution.py:181
  12.2 341.8 %reduce-scatter.3.cloned.1.call-start = ((), (), s32[]{:S(2)}) async-start(), calls=%async_computation.2 | async-start | bytes 2359296 | tf_op jit(solution)/shard_map/reduce_scatter | solution.py:185
  45.1 10.2 %collective-permute-start.10 = (bf16[192,512]{1,0:T(8,128)(2,1)S(1)}, bf16[192,512]{1,0:T(8,128)(2,1)S(1)}, u32[]{:S(2)}, u32[]{:S(2)}) collective-permute-start(bf16[192,512]{1,0:T(8,128)(2,1)S(1)} %get-tuple-element.139.refs_1_), channel_id=1, source_target_pairs={{0,8},{4,12},{8,0},{12,4},{1,9},{5,13},{9,1},{13,5},{2,10},{6,14},... | collective-permute-start | bytes 589832 | tf_op jit(solution)/shard_map/ppermute | solution.py:60
  62.2 10.7 %collective-permute-start.13 = (bf16[48,1024]{1,0:T(8,128)(2,1)S(1)}, bf16[48,1024]{1,0:T(8,128)(2,1)S(1)}, u32[]{:S(2)}, u32[]{:S(2)}) collective-permute-start(bf16[48,1024]{1,0:T(8,128)(2,1)S(1)} %get-tuple-element.142), channel_id=1, source_target_pairs={{0,2},{1,3},{2,0},{3,1},{4,6},{5,7},{6,4},{7,5},{8,10},{9,11},{10,... | collective-permute-start | bytes 294920 | tf_op jit(solution)/shard_map/ppermute | solution.py:60
  89.7 10.2 %collective-permute-start.19 = (bf16[48,1024]{1,0:T(8,128)(2,1)S(1)}, bf16[48,1024]{1,0:T(8,128)(2,1)S(1)}, u32[]{:S(2)}, u32[]{:S(2)}) collective-permute-start(bf16[48,1024]{1,0:T(8,128)(2,1)S(1)} %get-tuple-element.148), channel_id=1, source_target_pairs={{0,2},{1,3},{2,0},{3,1},{4,6},{5,7},{6,4},{7,5},{8,10},{9,11},{10,... | collective-permute-start | bytes 294920 | tf_op jit(solution)/shard_map/ppermute | solution.py:60
  115.5 11.2 %collective-permute-start.25 = (bf16[192,512]{1,0:T(8,128)(2,1)S(1)}, bf16[192,512]{1,0:T(8,128)(2,1)S(1)}, u32[]{:S(2)}, u32[]{:S(2)}) collective-permute-start(bf16[192,512]{1,0:T(8,128)(2,1)S(1)} %get-tuple-element.153.refs_1_), channel_id=1, source_target_pairs={{0,8},{4,12},{8,0},{12,4},{1,9},{5,13},{9,1},{13,5},{2,10},{6,14},... | collective-permute-start | bytes 589832 | tf_op jit(solution)/shard_map/ppermute | solution.py:60
  116.1 10.6 %collective-permute-start.24 = (bf16[192,512]{1,0:T(8,128)(2,1)S(1)}, bf16[192,512]{1,0:T(8,128)(2,1)S(1)}, u32[]{:S(2)}, u32[]{:S(2)}) collective-permute-start(bf16[192,512]{1,0:T(8,128)(2,1)S(1)} %get-tuple-element.153.refs_1_), channel_id=1, source_target_pairs={{0,4},{4,0},{8,12},{12,8},{1,5},{5,1},{9,13},{13,9},{2,6},{6,2},{1... | collective-permute-start | bytes 589832 | tf_op jit(solution)/shard_map/ppermute | solution.py:60
  130.7 10.9 %collective-permute-start.28 = (bf16[48,1024]{1,0:T(8,128)(2,1)S(1)}, bf16[48,1024]{1,0:T(8,128)(2,1)S(1)}, u32[]{:S(2)}, u32[]{:S(2)}) collective-permute-start(bf16[48,1024]{1,0:T(8,128)(2,1)S(1)} %get-tuple-element.156), channel_id=1, source_target_pairs={{0,2},{1,3},{2,0},{3,1},{4,6},{5,7},{6,4},{7,5},{8,10},{9,11},{10,... | collective-permute-start | bytes 294920 | tf_op jit(solution)/shard_map/ppermute | solution.py:60
  146.0 10.0 %collective-permute-start.31 = (bf16[48,1024]{1,0:T(8,128)(2,1)}, bf16[48,1024]{1,0:T(8,128)(2,1)}, u32[]{:S(2)}, u32[]{:S(2)}) collective-permute-start(bf16[48,1024]{1,0:T(8,128)(2,1)} %get-tuple-element.159.refs_0_), channel_id=1, source_target_pairs={{0,2},{1,3},{2,0},{3,1},{4,6},{5,7},{6,4},{7,5},{8,10},{9,11},{10,... | collective-permute-start | bytes 294920 | tf_op jit(solution)/shard_map/ppermute | solution.py:60
  161.4 10.3 %collective-permute-start.34 = (bf16[48,1024]{1,0:T(8,128)(2,1)S(1)}, bf16[48,1024]{1,0:T(8,128)(2,1)S(1)}, u32[]{:S(2)}, u32[]{:S(2)}) collective-permute-start(bf16[48,1024]{1,0:T(8,128)(2,1)S(1)} %get-tuple-element.162), channel_id=1, source_target_pairs={{0,2},{1,3},{2,0},{3,1},{4,6},{5,7},{6,4},{7,5},{8,10},{9,11},{10,... | collective-permute-start | bytes 294920 | tf_op jit(solution)/shard_map/ppermute | solution.py:60
  229.2 128.2 %reduce-scatter.5.cloned.1.call-start = ((), (), s32[]{:S(2)}) async-start(), calls=%async_computation.3 | async-start | bytes 4718592 | tf_op jit(solution)/shard_map/reduce_scatter | solution.py:185
  229.9 10.5 %collective-permute-start.51 = (bf16[48,1024]{1,0:T(8,128)(2,1)}, bf16[48,1024]{1,0:T(8,128)(2,1)S(1)}, u32[]{:S(2)}, u32[]{:S(2)}) collective-permute-start(bf16[48,1024]{1,0:T(8,128)(2,1)} %copy-done.94), channel_id=1, source_target_pairs={{0,2},{1,3},{2,0},{3,1},{4,6},{5,7},{6,4},{7,5},{8,10},{9,11},{10,... | collective-permute-start | bytes 294920 | tf_op jit(solution)/shard_map/ppermute | solution.py:60
  282.5 44.0 %collective-permute-start.77 = (bf16[4,2048,128]{2,1,0:T(8,128)(2,1)}, bf16[4,2048,128]{2,1,0:T(8,128)(2,1)}, u32[]{:S(2)}, u32[]{:S(2)}) collective-permute-start(bf16[4,2048,128]{2,1,0:T(8,128)(2,1)} %get-tuple-element.217), channel_id=1, source_target_pairs={{0,4},{4,0},{8,12},{12,8},{1,5},{5,1},{9,13},{13,9},{2,6},{6,2},{1... | collective-permute-start | bytes 6291464 | tf_op jit(solution)/shard_map/ppermute | solution.py:60
  296.7 24.1 %collective-permute-start.72 = (bf16[4,1056,128]{2,1,0:T(8,128)(2,1)S(1)}, bf16[4,1056,128]{2,1,0:T(8,128)(2,1)S(1)}, u32[]{:S(2)}, u32[]{:S(2)}) collective-permute-start(bf16[4,1056,128]{2,1,0:T(8,128)(2,1)S(1)} %get-tuple-element.246), channel_id=1, source_target_pairs={{0,4},{4,0},{8,12},{12,8},{1,5},{5,1},{9,13},{13,9},{2,6},{6,2},{1... | collective-permute-start | bytes 3244040 | tf_op jit(solution)/shard_map/ppermute | solution.py:60
  296.7 11.0 %collective-permute-start.65 = (bf16[48,1024]{1,0:T(8,128)(2,1)}, bf16[48,1024]{1,0:T(8,128)(2,1)S(1)}, u32[]{:S(2)}, u32[]{:S(2)}) collective-permute-start(bf16[48,1024]{1,0:T(8,128)(2,1)} %get-tuple-element.232), channel_id=1, source_target_pairs={{0,2},{1,3},{2,0},{3,1},{4,6},{5,7},{6,4},{7,5},{8,10},{9,11},{10,... | collective-permute-start | bytes 294920 | tf_op jit(solution)/shard_map/ppermute | solution.py:60
  303.8 12.1 %collective-permute-start.47 = (bf16[48,1024]{1,0:T(8,128)(2,1)S(1)}, bf16[48,1024]{1,0:T(8,128)(2,1)S(1)}, u32[]{:S(2)}, u32[]{:S(2)}) collective-permute-start(bf16[48,1024]{1,0:T(8,128)(2,1)S(1)} %copy-done.56), channel_id=1, source_target_pairs={{0,3},{1,2},{2,1},{3,0},{4,7},{5,6},{6,5},{7,4},{8,11},{9,10},{10,... | collective-permute-start | bytes 294920 | tf_op jit(solution)/shard_map/ppermute | solution.py:60
  307.8 10.5 %collective-permute-start.46 = (bf16[48,1024]{1,0:T(8,128)(2,1)S(1)}, bf16[48,1024]{1,0:T(8,128)(2,1)S(1)}, u32[]{:S(2)}, u32[]{:S(2)}) collective-permute-start(bf16[48,1024]{1,0:T(8,128)(2,1)S(1)} %copy-done.56), channel_id=1, source_target_pairs={{0,2},{1,3},{2,0},{3,1},{4,6},{5,7},{6,4},{7,5},{8,10},{9,11},{10,... | collective-permute-start | bytes 294920 | tf_op jit(solution)/shard_map/ppermute | solution.py:60
  307.8 10.5 %collective-permute-start.45 = (bf16[48,1024]{1,0:T(8,128)(2,1)S(1)}, bf16[48,1024]{1,0:T(8,128)(2,1)S(1)}, u32[]{:S(2)}, u32[]{:S(2)}) collective-permute-start(bf16[48,1024]{1,0:T(8,128)(2,1)S(1)} %copy-done.56), channel_id=1, source_target_pairs={{0,1},{1,0},{2,3},{3,2},{4,5},{5,4},{6,7},{7,6},{8,9},{9,8},{10,11... | collective-permute-start | bytes 294920 | tf_op jit(solution)/shard_map/ppermute | solution.py:60
  328.5 17.2 %collective-permute-start.78 = (bf16[2,1024,128]{2,1,0:T(8,128)(2,1)S(1)}, bf16[2,1024,128]{2,1,0:T(8,128)(2,1)S(1)}, u32[]{:S(2)}, u32[]{:S(2)}) collective-permute-start(bf16[2,1024,128]{2,1,0:T(8,128)(2,1)S(1)} %get-tuple-element.259), channel_id=1, source_target_pairs={{0,16},{16,0},{1,17},{17,1},{2,18},{18,2},{3,19},{19,3},{4,20},{20... | collective-permute-start | bytes 1572872 | tf_op jit(solution)/shard_map/ppermute | solution.py:60
  329.6 16.1 %collective-permute-start.79 = (bf16[2,1024,128]{2,1,0:T(8,128)(2,1)S(1)}, bf16[2,1024,128]{2,1,0:T(8,128)(2,1)S(1)}, u32[]{:S(2)}, u32[]{:S(2)}) collective-permute-start(bf16[2,1024,128]{2,1,0:T(8,128)(2,1)S(1)} %get-tuple-element.261), channel_id=1, source_target_pairs={{0,8},{4,12},{8,0},{12,4},{1,9},{5,13},{9,1},{13,5},{2,10},{6,14},... | collective-permute-start | bytes 1572872 | tf_op jit(solution)/shard_map/ppermute | solution.py:60
  330.9 14.7 %collective-permute-start.75 = (bf16[528,128]{1,0:T(8,128)(2,1)S(1)}, bf16[528,128]{1,0:T(8,128)(2,1)S(1)}, u32[]{:S(2)}, u32[]{:S(2)}) collective-permute-start(bf16[528,128]{1,0:T(8,128)(2,1)S(1)} %get-tuple-element.255), channel_id=1, source_target_pairs={{0,8},{4,12},{8,0},{12,4},{1,9},{5,13},{9,1},{13,5},{2,10},{6,14},... | collective-permute-start | bytes 405512 | tf_op jit(solution)/shard_map/ppermute | solution.py:60
  332.3 13.3 %collective-permute-start.76 = (bf16[528,128]{1,0:T(8,128)(2,1)S(1)}, bf16[528,128]{1,0:T(8,128)(2,1)S(1)}, u32[]{:S(2)}, u32[]{:S(2)}) collective-permute-start(bf16[528,128]{1,0:T(8,128)(2,1)S(1)} %get-tuple-element.257), channel_id=1, source_target_pairs={{0,16},{16,0},{1,17},{17,1},{2,18},{18,2},{3,19},{19,3},{4,20},{20... | collective-permute-start | bytes 405512 | tf_op jit(solution)/shard_map/ppermute | solution.py:60
  (168 other events, 991.1 us)
Sparse Core Ops, SparseCore 0:
  10.5 45.2 all-gather.6
  58.3 28.5 all-gather.8
  89.3 40.9 all-gather.10
  229.3 39.2 reduce-scatter.2
  272.2 55.8 reduce-scatter.4
